TPU v7x, 32 devices: a whole 2x2x4 slice. The times are simulated.
32 devices in a mesh: groups: 2 (over x), fsdp: 4 (over y, core), tensor: 4 (over z).
Axes of the slice: x: 2, y: 2, z: 4, core: 2. Of those that a mesh axis runs over, the one named last changes fastest.
Arguments:
- tokens: bfloat16 [8192, 5120], P(('groups', 'fsdp', 'tensor')), parts along dimension 0, may hold values from -6 to 6
- w_qkv: bfloat16 [10240, 6144], P(('groups', 'fsdp', 'tensor')), parts along dimension 0, may hold values from -0.078125 to 0.078125
- norm_gain: float32 [5120], replicated, may hold values from 0.1 to 1.9
- q_gain: float32 [128], replicated, may hold values from 0.5 to 3
- k_gain: float32 [128], replicated, may hold values from 0.5 to 3
- lengths: int32 [8], P(('groups', 'fsdp')), parts along dimension 0, may hold values from 256 to 1024, as said below
Outputs:
- attended: bfloat16 [8192, 4096], P(('groups', 'fsdp'), 'tensor'), parts along dimension 0
There are 2 independent parts, one for each index of `groups`. A program takes and returns all parts, laid end to end along the dimension named above; an argument that names none is the same for every part. Nothing has to cross between parts.
Inputs may be any that keep to these rules, and one draw needn't show every extreme that they name: `lengths`: one prompt has the full length 1024.
All inputs are finite; a program needn't handle non-finite values.
Results may differ from a plain program's by a relative error of at most 0.012.
The roundings to bfloat16 on the way count: a program that leaves them out, or rounds other values in their place, can miss the bound.
Values may be sent and summed in bfloat16 or wider, within the bound.
No kernel may reach another device: no remote copies, remote signals or barrier semaphores. Data moves between devices by JAX's collectives and lax.ppermute only.
A program may use at most 192 MiB of HBM per device.

v0:
```python
import jax
import jax.numpy as jnp
from jax import lax
from jax.sharding import PartitionSpec as P

KV = 8
HD = 128
GQ = 4


def head_norm(vec, gain):
    scale = lax.rsqrt(jnp.mean(vec * vec, axis=-1, keepdims=True) + 1e-06)
    return vec * scale * gain


def rotate(vec, positions):
    half = vec.shape[-1] // 2
    freqs = 1000000.0 ** (-2.0 * jnp.arange(half, dtype=jnp.float32) / vec.shape[-1])
    angle = positions.astype(jnp.float32)[:, None] * freqs[None, :]
    cosine = jnp.cos(angle)[:, None, None, :]
    sine = jnp.sin(angle)[:, None, None, :]
    first = vec[..., :half]
    second = vec[..., half:]
    return jnp.concatenate(
        [first * cosine - second * sine, second * cosine + first * sine], axis=-1
    )


def attend(qkv, q_gain, k_gain, length):
    rows = qkv.shape[0]
    group = qkv.shape[2] - 2
    positions = jnp.arange(rows, dtype=jnp.int32)
    query = rotate(head_norm(qkv[:, :, :group], q_gain), positions).astype(jnp.bfloat16)
    keyed = rotate(head_norm(qkv[:, :, group : group + 1], k_gain), positions)[:, :, 0].astype(
        jnp.bfloat16
    )
    value = qkv[:, :, group + 1].astype(jnp.bfloat16)
    scores = jnp.einsum(
        "ikgd,jkd->kgij", query, keyed, preferred_element_type=jnp.float32
    ) / jnp.sqrt(jnp.float32(qkv.shape[3]))
    allowed = (positions[None, :] <= positions[:, None]) & (positions[None, :] < length)
    scores = jnp.where(allowed[None, None], scores, jnp.float32(-1e30))
    top = jnp.max(scores, axis=-1, keepdims=True)
    weights = jnp.exp(scores - top)
    probs = (weights / jnp.sum(weights, axis=-1, keepdims=True)).astype(jnp.bfloat16)
    out = jnp.einsum("kgij,jkd->ikgd", probs, value, preferred_element_type=jnp.float32)
    return out.reshape(rows, -1).astype(jnp.bfloat16)


def per_device(tokens, w_qkv, norm_gain, q_gain, k_gain, lengths):
    tensor_count = lax.axis_size("tensor")
    fsdp_count = lax.axis_size("fsdp")
    local_rows = w_qkv.shape[0]
    columns = w_qkv.shape[1] // tensor_count
    gathered = lax.all_gather(w_qkv, "fsdp", axis=0, tiled=True)
    moved = lax.all_to_all(gathered, "tensor", split_axis=1, concat_axis=0, tiled=True)
    blocks = moved.reshape(tensor_count, fsdp_count, local_rows, columns)
    weight_cols = jnp.transpose(blocks, (1, 0, 2, 3)).reshape(
        fsdp_count * tensor_count * local_rows, columns
    )
    normed = head_norm(tokens.astype(jnp.float32), norm_gain).astype(jnp.bfloat16)
    qkv = jnp.dot(
        lax.all_gather(normed, "tensor", axis=0, tiled=True),
        weight_cols,
        preferred_element_type=jnp.float32,
    )
    kv_local = KV // tensor_count
    qkv = qkv.reshape(qkv.shape[0], kv_local, GQ + 2, HD)
    return attend(qkv, q_gain, k_gain, lengths[0])


def solution(mesh):
    placed = (
        P(("groups", "fsdp", "tensor"), None),
        P(("groups", "fsdp", "tensor"), None),
        P(),
        P(),
        P(),
        P(("groups", "fsdp")),
    )
    return jax.shard_map(
        per_device,
        mesh=mesh,
        in_specs=placed,
        out_specs=P(("groups", "fsdp"), "tensor"),
        check_vma=False,
    )
```

profile of v0, /device:TPU:24, one launch (start us, length us, event | category | flops | bytes accessed | tf_op | source)
XLA Modules:
  0.0 766.2 jit_solution(7661114530599911359)
XLA Ops:
  7.4 0.0 all-gather.5.cloned.1.call-start
  7.4 0.7 all-gather.5.cloned.1.call-update
  8.1 102.6 %all-gather.5.cloned.1.call-done = bf16[1280,6144]{1,0:T(8,128)(2,1)} async-done(((bf16[320,6144]{1,0:T(8,128)(2,1)}), bf16[1280,6144]{1,0:T(8,128)(2,1)}) %all-gather.5.cloned.1.call-update) | async-done | bytes 15728656 | tf_op jit(solution)/shard_map/all_gather | solution.py:55
  110.7 19.2 %copy.31 = bf16[1280,6144]{0,1:T(8,128)(2,1)} copy(bf16[1280,6144]{1,0:T(8,128)(2,1)} %all-gather.5.cloned.1.call-done) | data formatting | bytes 31457280 | tf_op jit(solution)/shard_map/all_gather | solution.py:55
  130.0 0.0 copy-start.1
  130.0 0.0 copy-start.2
  130.0 7.5 all-to-all-start
  137.5 0.0 all-gather.3.cloned.1.call-start
  137.5 0.0 copy-done.1
  137.5 0.6 fusion.8
  138.1 0.0 copy-done.2
  138.1 2.3 fusion.10
  140.4 0.0 all-gather.3.cloned.1.call-update
  141.1 1.0 multiply_cosine_fusion
  142.1 0.4 fusion.11
  142.5 502.3 %all-to-all-done = bf16[1280,4,1536]{0,2,1:T(8,128)(2,1)} async-done(((bf16[1280,4,1536]{0,2,1:T(8,128)(2,1)}), bf16[1280,4,1536]{0,2,1:T(8,128)(2,1)}, u32[]{:S(2)}, u32[]{:S(2)}) %all-to-all-start) | async-done | bytes 15728672 | tf_op jit(solution)/shard_map/all_to_all | solution.py:56
  644.8 20.6 %copy.32 = bf16[4,1280,1536]{2,1,0:T(8,128)(2,1)} copy(bf16[4,1280,1536]{1,2,0:T(8,128)(2,1)} %bitcast.3) | data formatting | bytes 31457280 | tf_op jit(solution)/shard_map/all_to_all | solution.py:56
  665.4 13.2 %copy.33 = bf16[4,4,320,1536]{3,2,1,0:T(8,128)(2,1)} copy(bf16[4,4,320,1536]{3,2,0,1:T(8,128)(2,1)} %bitcast.52) | data formatting | bytes 31457280 | tf_op jit(solution)/shard_map/transpose | solution.py:58
  678.7 20.7 %copy.34 = bf16[1536,5120]{1,0:T(8,128)(2,1)} copy(bf16[1536,5120]{0,1:T(8,128)(2,1)} %bitcast.53) | data formatting | bytes 31457280 | tf_op jit(solution)/shard_map/dot_general | solution.py:62
  699.4 0.0 all-gather.3.cloned.1.call-done
  699.4 20.1 %fusion.6 = f32[1024,2,6,128]{0,3,2,1:T(8,128)S(1)} fusion(bf16[2,6,128,5120]{3,2,1,0:T(8,128)(2,1)} %bitcast.54, bf16[1024,5120]{1,0:T(8,128)(2,1)} %all-gather.3.cloned.1.call-done), kind=kOutput, calls=%fused_computation.9 | convolution fusion | flops 16106127360 | bytes 32505856 | tf_op jit(solution)/shard_map/dot_general | solution.py:62
  719.5 0.0 copy-start
  719.5 0.0 copy-start.3
  719.6 0.0 copy-start.4
  719.6 0.1 multiply_reduce_fusion.1
  719.7 0.6 multiply_reduce_fusion
  720.3 0.0 copy-done.3
  720.3 0.2 multiply_multiply_fusion.1
  720.5 0.0 copy-done.4
  720.5 1.0 multiply_multiply_fusion
  721.5 1.0 copy-done
  722.5 0.2 subtract_convert_fusion.1
  722.7 1.7 subtract_convert_fusion
  724.4 19.6 %fusion.24 = (f32[2,4,1024]{2,1,0:T(4,128)S(1)}, f32[2,4,1024,1024]{2,3,1,0:T(8,128)}) fusion(pred[1024,1024]{0,1:T(8,128)(4,1)S(1)} %fusion.11, bf16[1024,2,4,64]{0,3,2,1:T(8,128)(2,1)} %get-tuple-element.6, bf16[1024,2,4,64]{0,3,2,1:T(8,128)(2,1)S(1)} %get-tuple-element.5, bf16[1024,2,1,64]{0,3,2,1:T(8,128)(2,1)S(1)} %get-tuple-element.8, ...), kind=kOutput, calls=%fused_computation.45 | convolution fusion | flops 2186281984 | bytes 37257216 | tf_op jit(solution)/shard_map/sub | solution.py:44
  744.0 12.2 %fusion.14 = bf16[2,128,4,1024]{3,1,2,0:T(8,128)(2,1)S(1)} fusion(f32[2,4,1024,1024]{2,3,1,0:T(8,128)} %get-tuple-element.12, f32[2,4,1024]{2,1,0:T(4,128)S(1)} %get-tuple-element.11, f32[1024,2,6,128]{0,3,2,1:T(8,128)} %copy-done), kind=kOutput, calls=%fused_computation.24 | convolution fusion | flops 2165309440 | bytes 36208640 | tf_op jit(solution)/shard_map/kgij,jkd->ikgd/dot_general | solution.py:46
  756.2 2.6 copy.38
  (6 shorter events, 0.1 us)
Async XLA Ops:
  7.4 103.4 %all-gather.5.cloned.1.call-start = ((), (), s32[]{:S(2)}) async-start(), calls=%async_computation.2 | async-start | bytes 19660800 | tf_op jit(solution)/shard_map/all_gather | solution.py:55
  130.0 7.5 copy-start.1
  130.0 8.1 %copy-start.2 = (f32[5120]{0:T(1024)S(1)}, f32[5120]{0:T(1024)}, u32[]{:S(2)}) copy-start(f32[5120]{0:T(1024)} %param.8) | copy-start | bytes 61444
  130.0 514.8 %all-to-all-start = ((bf16[1280,4,1536]{0,2,1:T(8,128)(2,1)}), bf16[1280,4,1536]{0,2,1:T(8,128)(2,1)}, u32[]{:S(2)}, u32[]{:S(2)}) async-start(bf16[1280,4,1536]{0,2,1:T(8,128)(2,1)} %bitcast.51), calls=%async_computation | async-start | bytes 31457280 | tf_op jit(solution)/shard_map/all_to_all | solution.py:56
  137.5 561.9 %all-gather.3.cloned.1.call-start = ((), (), s32[]{:S(2)}) async-start(), calls=%async_computation.1 | async-start | bytes 13107200 | tf_op jit(solution)/shard_map/all_gather | solution.py:63
  719.5 3.0 copy-start
  719.5 0.7 copy-start.3
  719.6 0.9 copy-start.4
Sparse Core Ops, SparseCore 0:
  9.7 100.9 all-gather.4
Sparse Core Ops, SparseCore 1:
  140.5 434.1 all-gather.2
where the time goes:
time: 772 us; the launch traced here: 766 us
  waiting for transfers between devices  606 us (78%)
  local copies, waits for them, and re-layouts  77.4 us (10%)
  matrix products  51.9 us (7%)
  between operations  15.6 us (2%)
  other arithmetic  8.02 us (1%)
    all_to_all x1, waiting for transfers between devices, per_device(): lax.all_to_all(gathered, 'tensor', split_axis=1, concat_axis=0, tiled=True)  502 us
    all_gather x1, waiting for transfers between devices, per_device(): gathered = lax.all_gather(w_qkv, 'fsdp', axis=0, tiled=True)  103 us
    dot_general x1, local copies, waits for them, and re-layouts, per_device(): jnp.dot(lax.all_gather(normed, 'tensor', axis=0, tiled=True), weight_cols...  20.7 us
    all_to_all x1, local copies, waits for them, and re-layouts, per_device(): lax.all_to_all(gathered, 'tensor', split_axis=1, concat_axis=0, tiled=True)  20.6 us
    dot_general x1, matrix products, per_device(): jnp.dot(lax.all_gather(normed, 'tensor', axis=0, tiled=True), weight_cols...  20.1 us
    sub x1, matrix products, attend(): weights = jnp.exp(scores - top)  19.6 us
    all_gather x1, local copies, waits for them, and re-layouts, per_device(): gathered = lax.all_gather(w_qkv, 'fsdp', axis=0, tiled=True)  19.2 us
  transfers between devices with their start and end apart: 3, of which 2 were waited for; matrix products, arithmetic and copies ran while one was open for 8% of the time, Pallas kernels for 0%

commit v1 on v0

--- a/solution.py
+++ b/solution.py
@@ -47,20 +47,65 @@
     return out.reshape(rows, -1).astype(jnp.bfloat16)
 
 
+def gather_weights(w_qkv):
+    tensor_count = lax.axis_size("tensor")
+    fsdp_count = lax.axis_size("fsdp")
+    t = lax.axis_index("tensor")
+    f = lax.axis_index("fsdp")
+    rows = w_qkv.shape[0]
+    columns = w_qkv.shape[1] // tensor_count
+    whole = jnp.zeros((fsdp_count, tensor_count, rows, columns), w_qkv.dtype)
+    for shift in range(tensor_count):
+        target = lax.rem(t + shift, tensor_count)
+        piece = lax.dynamic_slice(w_qkv, (0, target * columns), (rows, columns))
+        if shift:
+            piece = lax.ppermute(
+                piece,
+                "tensor",
+                [(i, (i + shift) % tensor_count) for i in range(tensor_count)],
+            )
+        source = lax.rem(t - shift + tensor_count, tensor_count)
+        held = [(0, piece)]
+        bit = fsdp_count // 2
+        while bit:
+            pairs = [(i, i ^ bit) for i in range(fsdp_count)]
+            held = held + [(m ^ bit, lax.ppermute(p, "fsdp", pairs)) for m, p in held]
+            bit //= 2
+        for m, p in held:
+            whole = lax.dynamic_update_slice(
+                whole, p[None, None], (jnp.bitwise_xor(f, m), source, 0, 0)
+            )
+    return whole.reshape(fsdp_count * tensor_count * rows, columns)
+
+
+def gather_rows(normed, chunks):
+    count = lax.axis_size("tensor")
+    t = lax.axis_index("tensor")
+    rows, width = normed.shape
+    part = rows // chunks
+    right = [(i, i + 1) for i in range(count - 1)]
+    left = [(i + 1, i) for i in range(count - 1)]
+    whole = jnp.zeros((count, rows, width), normed.dtype)
+    whole = lax.dynamic_update_slice(whole, normed[None], (t, 0, 0))
+    for c in range(chunks):
+        piece = normed[c * part : (c + 1) * part]
+        from_left, from_right = [piece], [piece]
+        for _ in range(count - 1):
+            from_left.append(lax.ppermute(from_left[-1], "tensor", right))
+            from_right.append(lax.ppermute(from_right[-1], "tensor", left))
+        for k in range(1, count):
+            block = jnp.where(t >= k, from_left[k], from_right[count - k])
+            source = lax.rem(t - k + count, count)
+            whole = lax.dynamic_update_slice(whole, block[None], (source, c * part, 0))
+    return whole.reshape(count * rows, width)
+
+
 def per_device(tokens, w_qkv, norm_gain, q_gain, k_gain, lengths):
     tensor_count = lax.axis_size("tensor")
-    fsdp_count = lax.axis_size("fsdp")
-    local_rows = w_qkv.shape[0]
-    columns = w_qkv.shape[1] // tensor_count
-    gathered = lax.all_gather(w_qkv, "fsdp", axis=0, tiled=True)
-    moved = lax.all_to_all(gathered, "tensor", split_axis=1, concat_axis=0, tiled=True)
-    blocks = moved.reshape(tensor_count, fsdp_count, local_rows, columns)
-    weight_cols = jnp.transpose(blocks, (1, 0, 2, 3)).reshape(
-        fsdp_count * tensor_count * local_rows, columns
-    )
+    weight_cols = gather_weights(w_qkv)
     normed = head_norm(tokens.astype(jnp.float32), norm_gain).astype(jnp.bfloat16)
     qkv = jnp.dot(
-        lax.all_gather(normed, "tensor", axis=0, tiled=True),
+        gather_rows(normed, 2),
         weight_cols,
         preferred_element_type=jnp.float32,
     )

time: 772 us -> 346 us (0.45)
  waiting for transfers between devices: 606 us -> 169 us
  starting transfers between devices: 7.53 us -> 35.5 us
  local copies, waits for them, and re-layouts: 77.4 us -> 60.6 us
  other arithmetic: 8.02 us -> 23.5 us
  between operations: 15.6 us -> 1.02 us
    all_to_all x1 -> x0, waiting for transfers between devices: 502 us -> none  [per_device(): lax.all_to_all(gathered, 'tensor', split_axis=1, concat_axis=0, tiled=True)]
    ppermute x0 -> x27, waiting for transfers between devices: none -> 169 us  [the longest x3 67.7 us: gather_weights(): lax.ppermute(piece, 'tensor', [(i, (i + shift) % tensor_count) for i in r...]
    all_gather x2 -> x0, waiting for transfers between devices: 103 us -> none  [the longest x1 103 us: per_device(): gathered = lax.all_gather(w_qkv, 'fsdp', axis=0, tiled=True)]
    ppermute x0 -> x27, starting transfers between devices: none -> 35.5 us  [the longest x6 22.1 us: gather_rows(): from_right.append(lax.ppermute(from_right[-1], 'tensor', left))]
    dynamic_update_slice x0 -> x16, local copies, waits for them, and re-layouts: none -> 21.6 us  [gather_weights(): lax.dynamic_update_slice(whole, p[None, None], (jnp.bitwise_xor(f, m), so...]
    all_to_all x1 -> x0, local copies, waits for them, and re-layouts: 20.6 us -> none  [per_device(): lax.all_to_all(gathered, 'tensor', split_axis=1, concat_axis=0, tiled=True)]
    all_gather x1 -> x0, local copies, waits for them, and re-layouts: 19.2 us -> none  [per_device(): gathered = lax.all_gather(w_qkv, 'fsdp', axis=0, tiled=True)]
    dynamic_update_slice x0 -> x7, other arithmetic: none -> 16.8 us  [the longest x6 15.9 us: gather_rows(): whole = lax.dynamic_update_slice(whole, block[None], (source, c * part, 0))]
  transfers between devices with their start and end apart: 3 -> 27, of which waited for: 2 -> 13; matrix products, arithmetic and copies ran while one was open for 8% -> 18% of each run, Pallas kernels for 0% -> 0%
where the time goes in v1:
time: 346 us; the launch traced here: 345 us
  waiting for transfers between devices  169 us (49%)
  local copies, waits for them, and re-layouts  60.6 us (18%)
  matrix products  55.4 us (16%)
  starting transfers between devices  35.5 us (10%)
  other arithmetic  23.5 us (7%)
    ppermute x3, waiting for transfers between devices, gather_weights(): lax.ppermute(piece, 'tensor', [(i, (i + shift) % tensor_count) for i in r...  67.7 us
    ppermute x12, waiting for transfers between devices, gather_weights(): held = held + [(m ^ bit, lax.ppermute(p, 'fsdp', pairs)) for m, p in held]  49.3 us
    ppermute x6, waiting for transfers between devices, gather_rows(): from_right.append(lax.ppermute(from_right[-1], 'tensor', left))  37.2 us
    dot_general x1, matrix products, per_device(): jnp.dot(gather_rows(normed, 2), weight_cols, preferred_element_type=jnp.f...  23.6 us
    ppermute x6, starting transfers between devices, gather_rows(): from_right.append(lax.ppermute(from_right[-1], 'tensor', left))  22.1 us
    dynamic_update_slice x16, local copies, waits for them, and re-layouts, gather_weights(): lax.dynamic_update_slice(whole, p[None, None], (jnp.bitwise_xor(f, m), so...  21.6 us
    dot_general x1, local copies, waits for them, and re-layouts, per_device(): jnp.dot(gather_rows(normed, 2), weight_cols, preferred_element_type=jnp.f...  20.7 us
    sub x1, matrix products, attend(): weights = jnp.exp(scores - top)  19.6 us
  transfers between devices with their start and end apart: 27, of which 13 were waited for; matrix products, arithmetic and copies ran while one was open for 18% of the time, Pallas kernels for 0%

profile of v1, /device:TPU:24, one launch (start us, length us, event | category | flops | bytes accessed | tf_op | source)
XLA Modules:
  0.0 345.4 jit_solution(14176611903897837688)
XLA Ops:
  0.0 7.0 %broadcast_in_dim.115 = bf16[4,4,320,1536]{3,2,1,0:T(8,128)(2,1)} broadcast(bf16[]{:T(256)} %constant.56.clone.1), dimensions={} | broadcast | bytes 15728642 | tf_op jit(solution)/shard_map/broadcast_in_dim | solution.py:57
  7.0 2.6 bitcast_dynamic-update-slice_fusion.22
  9.6 1.5 collective-permute-start.12
  11.1 3.5 %constant_dynamic-slice_fusion = (bf16[320,1536]{1,0:T(8,128)(2,1)}, bf16[320,1536]{1,0:T(8,128)(2,1)}, bf16[320,1536]{1,0:T(8,128)(2,1)}) fusion(bf16[320,6144]{1,0:T(8,128)(2,1)} %param.7, s32[]{:T(128)S(6)} %select_n.126, s32[]{:T(128)S(6)} %select_n.124, s32[]{:T(128)S(6)} %select_n.125), kind=kLoop, calls=%fused_computation.58 | loop fusion | bytes 5898252 | tf_op jit(solution)/shard_map/dynamic_slice | solution.py:60
  14.9 0.6 fusion.6
  15.5 1.3 broadcast_in_dim.107
  16.8 0.9 bitcast_dynamic-update-slice_fusion
  17.9 3.7 %copy-done.3 = bf16[4,256,5120]{2,1,0:T(8,128)(2,1)} copy-done((bf16[4,256,5120]{2,1,0:T(8,128)(2,1)}, bf16[4,256,5120]{2,1,0:T(8,128)(2,1)S(1)}, u32[]{:S(2)}) %copy-start.3) | copy-done | bytes 10485784
  21.6 4.8 %collective-permute-start.1 = (bf16[128,5120]{1,0:T(8,128)(2,1)S(1)}, bf16[128,5120]{1,0:T(8,128)(2,1)}, u32[]{:S(2)}, u32[]{:S(2)}) collective-permute-start(bf16[128,5120]{1,0:T(8,128)(2,1)S(1)} %get-tuple-element.15), channel_id=1, source_target_pairs={{1,0},{2,1},{3,2},{5,4},{6,5},{7,6},{9,8},{10,9},{11,10},{13,12},{... | collective-permute-start | bytes 3932168 | tf_op jit(solution)/shard_map/ppermute | solution.py:95
  26.4 1.3 collective-permute-start
  27.7 1.0 multiply_cosine_fusion
  29.4 1.3 fusion.9
  30.7 2.7 collective-permute-done.12
  33.5 6.1 %collective-permute-done.15 = bf16[320,1536]{1,0:T(8,128)(2,1)} collective-permute-done((bf16[320,1536]{1,0:T(8,128)(2,1)}, bf16[320,1536]{1,0:T(8,128)(2,1)}, u32[]{:S(2)}, u32[]{:S(2)}) %collective-permute-start.15) | collective-permute-done | bytes 983072 | tf_op jit(solution)/shard_map/ppermute | solution.py:62
  40.0 2.2 bitcast_dynamic-update-slice_fusion.21
  42.7 2.2 bitcast_dynamic-update-slice_fusion.20
  44.9 17.8 %collective-permute-done.16 = bf16[320,1536]{1,0:T(8,128)(2,1)S(1)} collective-permute-done((bf16[320,1536]{1,0:T(8,128)(2,1)}, bf16[320,1536]{1,0:T(8,128)(2,1)S(1)}, u32[]{:S(2)}, u32[]{:S(2)}) %collective-permute-start.16) | collective-permute-done | bytes 983072 | tf_op jit(solution)/shard_map/ppermute | solution.py:72
  62.7 1.0 bitcast_dynamic-update-slice_fusion.19
  63.8 2.2 bitcast_dynamic-update-slice_fusion.18
  66.0 1.0 bitcast_dynamic-update-slice_fusion.17
  67.5 1.0 bitcast_dynamic-update-slice_fusion.16
  68.6 61.6 %collective-permute-done.19 = bf16[320,1536]{1,0:T(8,128)(2,1)S(1)} collective-permute-done((bf16[320,1536]{1,0:T(8,128)(2,1)}, bf16[320,1536]{1,0:T(8,128)(2,1)S(1)}, u32[]{:S(2)}, u32[]{:S(2)}) %collective-permute-start.19) | collective-permute-done | bytes 983072 | tf_op jit(solution)/shard_map/ppermute | solution.py:62
  130.2 1.4 collective-permute-start.7
  132.2 1.0 bitcast_dynamic-update-slice_fusion.15
  133.2 1.3 collective-permute-start.6
  134.5 1.0 bitcast_dynamic-update-slice_fusion.14
  135.6 1.6 collective-permute-start.24
  137.2 19.1 %collective-permute-done.20 = bf16[320,1536]{1,0:T(8,128)(2,1)S(1)} collective-permute-done((bf16[320,1536]{1,0:T(8,128)(2,1)S(1)}, bf16[320,1536]{1,0:T(8,128)(2,1)S(1)}, u32[]{:S(2)}, u32[]{:S(2)}) %collective-permute-start.20) | collective-permute-done | bytes 983072 | tf_op jit(solution)/shard_map/ppermute | solution.py:72
  156.3 1.1 bitcast_dynamic-update-slice_fusion.13
  157.4 2.7 collective-permute-start.2
  160.1 1.0 bitcast_dynamic-update-slice_fusion.12
  161.4 3.8 %collective-permute-done.6 = bf16[128,5120]{1,0:T(8,128)(2,1)S(1)} collective-permute-done((bf16[128,5120]{1,0:T(8,128)(2,1)S(1)}, bf16[128,5120]{1,0:T(8,128)(2,1)S(1)}, u32[]{:S(2)}, u32[]{:S(2)}) %collective-permute-start.6) | collective-permute-done | bytes 1310752 | tf_op jit(solution)/shard_map/ppermute | solution.py:94
  165.2 1.3 collective-permute-start.4
  166.5 9.6 %collective-permute-done.24 = bf16[320,1536]{1,0:T(8,128)(2,1)S(1)} collective-permute-done((bf16[320,1536]{1,0:T(8,128)(2,1)S(1)}, bf16[320,1536]{1,0:T(8,128)(2,1)S(1)}, u32[]{:S(2)}, u32[]{:S(2)}) %collective-permute-start.24) | collective-permute-done | bytes 983072 | tf_op jit(solution)/shard_map/ppermute | solution.py:72
  176.1 2.4 collective-permute-start.8
  178.6 1.3 collective-permute-start.10
  179.9 1.1 bitcast_dynamic-update-slice_fusion.11
  180.9 1.0 bitcast_dynamic-update-slice_fusion.10
  182.0 7.4 %collective-permute-done.2 = bf16[128,5120]{1,0:T(8,128)(2,1)S(1)} collective-permute-done((bf16[128,5120]{1,0:T(8,128)(2,1)}, bf16[128,5120]{1,0:T(8,128)(2,1)S(1)}, u32[]{:S(2)}, u32[]{:S(2)}) %collective-permute-start.2) | collective-permute-done | bytes 1310752 | tf_op jit(solution)/shard_map/ppermute | solution.py:95
  189.4 5.3 %collective-permute-start.3 = (bf16[128,5120]{1,0:T(8,128)(2,1)S(1)}, bf16[128,5120]{1,0:T(8,128)(2,1)}, u32[]{:S(2)}, u32[]{:S(2)}) collective-permute-start(bf16[128,5120]{1,0:T(8,128)(2,1)S(1)} %collective-permute-done.2), channel_id=1, source_target_pairs={{1,0},{2,1},{3,2},{5,4},{6,5},{7,6},{9,8},{10,9},{11,10},{13,12},{... | collective-permute-start | bytes 3932168 | tf_op jit(solution)/shard_map/ppermute | solution.py:95
  194.7 1.0 bitcast_dynamic-update-slice_fusion.9
  195.7 3.3 collective-permute-done.4
  199.1 1.3 collective-permute-start.5
  200.4 17.0 %collective-permute-done.8 = bf16[128,5120]{1,0:T(8,128)(2,1)S(1)} collective-permute-done((bf16[128,5120]{1,0:T(8,128)(2,1)S(1)}, bf16[128,5120]{1,0:T(8,128)(2,1)S(1)}, u32[]{:S(2)}, u32[]{:S(2)}) %collective-permute-start.8) | collective-permute-done | bytes 1310752 | tf_op jit(solution)/shard_map/ppermute | solution.py:95
  217.4 5.4 %collective-permute-start.9 = (bf16[128,5120]{1,0:T(8,128)(2,1)S(1)}, bf16[128,5120]{1,0:T(8,128)(2,1)}, u32[]{:S(2)}, u32[]{:S(2)}) collective-permute-start(bf16[128,5120]{1,0:T(8,128)(2,1)S(1)} %collective-permute-done.8), channel_id=1, source_target_pairs={{1,0},{2,1},{3,2},{5,4},{6,5},{7,6},{9,8},{10,9},{11,10},{13,12},{... | collective-permute-start | bytes 3932168 | tf_op jit(solution)/shard_map/ppermute | solution.py:95
  222.8 4.4 %collective-permute-done.10 = bf16[128,5120]{1,0:T(8,128)(2,1)} collective-permute-done((bf16[128,5120]{1,0:T(8,128)(2,1)S(1)}, bf16[128,5120]{1,0:T(8,128)(2,1)}, u32[]{:S(2)}, u32[]{:S(2)}) %collective-permute-start.10) | collective-permute-done | bytes 1310752 | tf_op jit(solution)/shard_map/ppermute | solution.py:94
  227.2 1.3 collective-permute-start.11
  228.5 1.0 bitcast_dynamic-update-slice_fusion.8
  229.5 1.0 bitcast_dynamic-update-slice_fusion.7
  230.5 20.7 %copy.16 = bf16[1536,5120]{1,0:T(8,128)(2,1)} copy(bf16[1536,5120]{0,1:T(8,128)(2,1)} %bitcast.93) | data formatting | bytes 31457280 | tf_op jit(solution)/shard_map/dot_general | solution.py:107
  251.2 2.9 bitcast_dynamic-update-slice_fusion.6
  254.1 2.8 bitcast_dynamic-update-slice_fusion.5
  256.9 3.5 %bitcast_dynamic-update-slice_fusion.4 = bf16[4,256,5120]{2,1,0:T(8,128)(2,1)} fusion(bf16[4,256,5120]{2,1,0:T(8,128)(2,1)} %bitcast_dynamic-update-slice_fusion.5, s32[]{:T(128)S(6)} %select_n.114, bf16[128,5120]{1,0:T(8,128)(2,1)} %collective-permute-done.5, bf16[128,5120]{1,0:T(8,128)(2,1)} %collective-permute-done.1, pred[]{:T(512)S(6)} %ge.14), kind=kLoop, calls=%fused_computation.28 | loop fusion | flops 655360 | bytes 3932165 | tf_op jit(solution)/shard_map/dynamic_update_slice | solution.py:99
  260.4 12.8 %collective-permute-done.9 = bf16[128,5120]{1,0:T(8,128)(2,1)} collective-permute-done((bf16[128,5120]{1,0:T(8,128)(2,1)S(1)}, bf16[128,5120]{1,0:T(8,128)(2,1)}, u32[]{:S(2)}, u32[]{:S(2)}) %collective-permute-start.9) | collective-permute-done | bytes 1310752 | tf_op jit(solution)/shard_map/ppermute | solution.py:95
  273.2 1.4 bitcast_dynamic-update-slice_fusion.3
  274.5 2.7 bitcast_dynamic-update-slice_fusion.2
  277.2 3.6 %collective-permute-done.11 = bf16[128,5120]{1,0:T(8,128)(2,1)} collective-permute-done((bf16[128,5120]{1,0:T(8,128)(2,1)}, bf16[128,5120]{1,0:T(8,128)(2,1)}, u32[]{:S(2)}, u32[]{:S(2)}) %collective-permute-start.11) | collective-permute-done | bytes 1310752 | tf_op jit(solution)/shard_map/ppermute | solution.py:94
  280.8 2.7 bitcast_dynamic-update-slice_fusion.1
  283.5 23.6 %fusion.25 = f32[1024,2,6,128]{0,3,2,1:T(8,128)S(1)} fusion(bf16[1024,5120,1,1]{1,0,3,2:T(8,128)(2,1)} %bitcast.95, bf16[2,6,128,5120]{3,2,1,0:T(8,128)(2,1)S(1)} %bitcast.94), kind=kOutput, calls=%fused_computation.72 | convolution fusion | flops 16106127360 | bytes 32505856 | tf_op jit(solution)/shard_map/dot_general | solution.py:107
  308.0 1.0 multiply_multiply_fusion
  309.2 1.7 subtract_convert_fusion
  311.0 19.6 %fusion.24 = (f32[2,4,1024]{2,1,0:T(4,128)S(1)}, f32[2,4,1024,1024]{2,3,1,0:T(8,128)}) fusion(pred[1024,1024]{0,1:T(8,128)(4,1)S(1)} %copy-done.8, bf16[1024,2,4,64]{0,3,2,1:T(8,128)(2,1)} %get-tuple-element.10, bf16[1024,2,4,64]{0,3,2,1:T(8,128)(2,1)S(1)} %get-tuple-element.9, bf16[1024,2,1,64]{0,3,2,1:T(8,128)(2,1)S(1)} %get-tuple-element.17, ...), kind=kOutput, calls=%fused_computation.71 | convolution fusion | flops 2186281984 | bytes 37257216 | tf_op jit(solution)/shard_map/sub | solution.py:44
  330.6 12.2 %fusion.12 = bf16[2,128,4,1024]{3,1,2,0:T(8,128)(2,1)S(1)} fusion(f32[2,4,1024,1024]{2,3,1,0:T(8,128)} %get-tuple-element.21, f32[2,4,1024]{2,1,0:T(4,128)S(1)} %get-tuple-element.20, f32[1024,2,6,128]{0,3,2,1:T(8,128)} %copy-done), kind=kOutput, calls=%fused_computation.23 | convolution fusion | flops 2165309440 | bytes 36208640 | tf_op jit(solution)/shard_map/kgij,jkd->ikgd/dot_general | solution.py:46
  342.8 2.6 copy.20
  (63 shorter events, 4.0 us)
Async XLA Ops:
  0.0 14.9 %copy-start.2 = (bf16[256,5120]{1,0:T(8,128)(2,1)S(1)}, bf16[256,5120]{1,0:T(8,128)(2,1)}, u32[]{:S(2)}) copy-start(bf16[256,5120]{1,0:T(8,128)(2,1)} %param.6) | copy-start | bytes 7864324
  7.0 9.8 %copy-start.10 = (f32[5120]{0:T(1024)S(1)}, f32[5120]{0:T(1024)}, u32[]{:S(2)}) copy-start(f32[5120]{0:T(1024)} %param.8) | copy-start | bytes 61444
  9.6 23.8 %collective-permute-start.12 = (bf16[320,1536]{1,0:T(8,128)(2,1)}, bf16[320,1536]{1,0:T(8,128)(2,1)}, u32[]{:S(2)}, u32[]{:S(2)}) collective-permute-start(bf16[320,1536]{1,0:T(8,128)(2,1)} %get-tuple-element.6), channel_id=1, source_target_pairs={{0,8},{4,12},{8,0},{12,4},{1,9},{5,13},{9,1},{13,5},{2,10},{6,14},... | collective-permute-start | bytes 2949128 | tf_op jit(solution)/shard_map/ppermute | solution.py:72
  11.1 31.1 %collective-permute-start.13 = (bf16[320,1536]{1,0:T(8,128)(2,1)}, bf16[320,1536]{1,0:T(8,128)(2,1)}, u32[]{:S(2)}, u32[]{:S(2)}) collective-permute-start(bf16[320,1536]{1,0:T(8,128)(2,1)} %get-tuple-element.6), channel_id=1, source_target_pairs={{0,4},{4,0},{8,12},{12,8},{1,5},{5,1},{9,13},{13,9},{2,6},{6,2},{1... | collective-permute-start | bytes 2949128 | tf_op jit(solution)/shard_map/ppermute | solution.py:72
  14.6 24.9 %collective-permute-start.15 = (bf16[320,1536]{1,0:T(8,128)(2,1)}, bf16[320,1536]{1,0:T(8,128)(2,1)}, u32[]{:S(2)}, u32[]{:S(2)}) collective-permute-start(bf16[320,1536]{1,0:T(8,128)(2,1)} %get-tuple-element.12), channel_id=1, source_target_pairs={{0,1},{1,2},{2,3},{3,0},{4,5},{5,6},{6,7},{7,4},{8,9},{9,10},{10,1... | collective-permute-start | bytes 2949128 | tf_op jit(solution)/shard_map/ppermute | solution.py:62
  17.7 3.9 %copy-start.3 = (bf16[4,256,5120]{2,1,0:T(8,128)(2,1)}, bf16[4,256,5120]{2,1,0:T(8,128)(2,1)S(1)}, u32[]{:S(2)}) copy-start(bf16[4,256,5120]{2,1,0:T(8,128)(2,1)S(1)} %get-tuple-element.7) | copy-start | bytes 31457284
  21.6 112.8 %collective-permute-start.1 = (bf16[128,5120]{1,0:T(8,128)(2,1)S(1)}, bf16[128,5120]{1,0:T(8,128)(2,1)}, u32[]{:S(2)}, u32[]{:S(2)}) collective-permute-start(bf16[128,5120]{1,0:T(8,128)(2,1)S(1)} %get-tuple-element.15), channel_id=1, source_target_pairs={{1,0},{2,1},{3,2},{5,4},{6,5},{7,6},{9,8},{10,9},{11,10},{13,12},{... | collective-permute-start | bytes 3932168 | tf_op jit(solution)/shard_map/ppermute | solution.py:95
  26.4 109.2 %collective-permute-start = (bf16[128,5120]{1,0:T(8,128)(2,1)S(1)}, bf16[128,5120]{1,0:T(8,128)(2,1)}, u32[]{:S(2)}, u32[]{:S(2)}) collective-permute-start(bf16[128,5120]{1,0:T(8,128)(2,1)S(1)} %get-tuple-element.15), channel_id=1, source_target_pairs={{0,1},{1,2},{2,3},{4,5},{5,6},{6,7},{8,9},{9,10},{10,11},{12,13},{... | collective-permute-start | bytes 3932168 | tf_op jit(solution)/shard_map/ppermute | solution.py:94
  29.4 37.6 %copy-start.9 = (bf16[320,1536]{1,0:T(8,128)(2,1)S(1)}, bf16[320,1536]{1,0:T(8,128)(2,1)}, u32[]{:S(2)}) copy-start(bf16[320,1536]{1,0:T(8,128)(2,1)} %get-tuple-element.11) | copy-start | bytes 2949124
  33.5 11.5 %collective-permute-start.14 = (bf16[320,1536]{1,0:T(8,128)(2,1)}, bf16[320,1536]{1,0:T(8,128)(2,1)S(1)}, u32[]{:S(2)}, u32[]{:S(2)}) collective-permute-start(bf16[320,1536]{1,0:T(8,128)(2,1)} %collective-permute-done.12), channel_id=1, source_target_pairs={{0,4},{4,0},{8,12},{12,8},{1,5},{5,1},{9,13},{13,9},{2,6},{6,2},{1... | collective-permute-start | bytes 2949128 | tf_op jit(solution)/shard_map/ppermute | solution.py:72
  39.5 23.2 %collective-permute-start.16 = (bf16[320,1536]{1,0:T(8,128)(2,1)}, bf16[320,1536]{1,0:T(8,128)(2,1)S(1)}, u32[]{:S(2)}, u32[]{:S(2)}) collective-permute-start(bf16[320,1536]{1,0:T(8,128)(2,1)} %collective-permute-done.15), channel_id=1, source_target_pairs={{0,8},{4,12},{8,0},{12,4},{1,9},{5,13},{9,1},{13,5},{2,10},{6,14},... | collective-permute-start | bytes 2949128 | tf_op jit(solution)/shard_map/ppermute | solution.py:72
  42.2 88.0 %collective-permute-start.19 = (bf16[320,1536]{1,0:T(8,128)(2,1)}, bf16[320,1536]{1,0:T(8,128)(2,1)S(1)}, u32[]{:S(2)}, u32[]{:S(2)}) collective-permute-start(bf16[320,1536]{1,0:T(8,128)(2,1)} %get-tuple-element.13), channel_id=1, source_target_pairs={{0,2},{1,3},{2,0},{3,1},{4,6},{5,7},{6,4},{7,5},{8,10},{9,11},{10,... | collective-permute-start | bytes 2949128 | tf_op jit(solution)/shard_map/ppermute | solution.py:62
  44.9 22.0 %collective-permute-start.17 = (bf16[320,1536]{1,0:T(8,128)(2,1)}, bf16[320,1536]{1,0:T(8,128)(2,1)S(1)}, u32[]{:S(2)}, u32[]{:S(2)}) collective-permute-start(bf16[320,1536]{1,0:T(8,128)(2,1)} %collective-permute-done.15), channel_id=1, source_target_pairs={{0,4},{4,0},{8,12},{12,8},{1,5},{5,1},{9,13},{13,9},{2,6},{6,2},{1... | collective-permute-start | bytes 2949128 | tf_op jit(solution)/shard_map/ppermute | solution.py:72
  62.7 68.8 %collective-permute-start.18 = (bf16[320,1536]{1,0:T(8,128)(2,1)S(1)}, bf16[320,1536]{1,0:T(8,128)(2,1)S(1)}, u32[]{:S(2)}, u32[]{:S(2)}) collective-permute-start(bf16[320,1536]{1,0:T(8,128)(2,1)S(1)} %collective-permute-done.16), channel_id=1, source_target_pairs={{0,4},{4,0},{8,12},{12,8},{1,5},{5,1},{9,13},{13,9},{2,6},{6,2},{1... | collective-permute-start | bytes 2949128 | tf_op jit(solution)/shard_map/ppermute | solution.py:72
  67.0 66.2 %collective-permute-start.23 = (bf16[320,1536]{1,0:T(8,128)(2,1)S(1)}, bf16[320,1536]{1,0:T(8,128)(2,1)S(1)}, u32[]{:S(2)}, u32[]{:S(2)}) collective-permute-start(bf16[320,1536]{1,0:T(8,128)(2,1)S(1)} %copy-done.9), channel_id=1, source_target_pairs={{0,3},{1,0},{2,1},{3,2},{4,7},{5,4},{6,5},{7,6},{8,11},{9,8},{10,9... | collective-permute-start | bytes 2949128 | tf_op jit(solution)/shard_map/ppermute | solution.py:62
  130.2 30.9 %collective-permute-start.7 = (bf16[128,5120]{1,0:T(8,128)(2,1)S(1)}, bf16[128,5120]{1,0:T(8,128)(2,1)S(1)}, u32[]{:S(2)}, u32[]{:S(2)}) collective-permute-start(bf16[128,5120]{1,0:T(8,128)(2,1)S(1)} %get-tuple-element.14), channel_id=1, source_target_pairs={{1,0},{2,1},{3,2},{5,4},{6,5},{7,6},{9,8},{10,9},{11,10},{13,12},{... | collective-permute-start | bytes 3932168 | tf_op jit(solution)/shard_map/ppermute | solution.py:95
  131.6 24.7 %collective-permute-start.20 = (bf16[320,1536]{1,0:T(8,128)(2,1)S(1)}, bf16[320,1536]{1,0:T(8,128)(2,1)S(1)}, u32[]{:S(2)}, u32[]{:S(2)}) collective-permute-start(bf16[320,1536]{1,0:T(8,128)(2,1)S(1)} %collective-permute-done.19), channel_id=1, source_target_pairs={{0,8},{4,12},{8,0},{12,4},{1,9},{5,13},{9,1},{13,5},{2,10},{6,14},... | collective-permute-start | bytes 2949128 | tf_op jit(solution)/shard_map/ppermute | solution.py:72
  133.2 32.0 %collective-permute-start.6 = (bf16[128,5120]{1,0:T(8,128)(2,1)S(1)}, bf16[128,5120]{1,0:T(8,128)(2,1)S(1)}, u32[]{:S(2)}, u32[]{:S(2)}) collective-permute-start(bf16[128,5120]{1,0:T(8,128)(2,1)S(1)} %get-tuple-element.14), channel_id=1, source_target_pairs={{0,1},{1,2},{2,3},{4,5},{5,6},{6,7},{8,9},{9,10},{10,11},{12,13},{... | collective-permute-start | bytes 3932168 | tf_op jit(solution)/shard_map/ppermute | solution.py:94
  134.5 22.9 %collective-permute-start.21 = (bf16[320,1536]{1,0:T(8,128)(2,1)S(1)}, bf16[320,1536]{1,0:T(8,128)(2,1)S(1)}, u32[]{:S(2)}, u32[]{:S(2)}) collective-permute-start(bf16[320,1536]{1,0:T(8,128)(2,1)S(1)} %collective-permute-done.19), channel_id=1, source_target_pairs={{0,4},{4,0},{8,12},{12,8},{1,5},{5,1},{9,13},{13,9},{2,6},{6,2},{1... | collective-permute-start | bytes 2949128 | tf_op jit(solution)/shard_map/ppermute | solution.py:72
  135.6 40.5 %collective-permute-start.24 = (bf16[320,1536]{1,0:T(8,128)(2,1)S(1)}, bf16[320,1536]{1,0:T(8,128)(2,1)S(1)}, u32[]{:S(2)}, u32[]{:S(2)}) collective-permute-start(bf16[320,1536]{1,0:T(8,128)(2,1)S(1)} %collective-permute-done.23), channel_id=1, source_target_pairs={{0,8},{4,12},{8,0},{12,4},{1,9},{5,13},{9,1},{13,5},{2,10},{6,14},... | collective-permute-start | bytes 2949128 | tf_op jit(solution)/shard_map/ppermute | solution.py:72
  156.3 22.3 %collective-permute-start.22 = (bf16[320,1536]{1,0:T(8,128)(2,1)S(1)}, bf16[320,1536]{1,0:T(8,128)(2,1)S(1)}, u32[]{:S(2)}, u32[]{:S(2)}) collective-permute-start(bf16[320,1536]{1,0:T(8,128)(2,1)S(1)} %collective-permute-done.20), channel_id=1, source_target_pairs={{0,4},{4,0},{8,12},{12,8},{1,5},{5,1},{9,13},{13,9},{2,6},{6,2},{1... | collective-permute-start | bytes 2949128 | tf_op jit(solution)/shard_map/ppermute | solution.py:72
  157.4 32.0 %collective-permute-start.2 = (bf16[128,5120]{1,0:T(8,128)(2,1)}, bf16[128,5120]{1,0:T(8,128)(2,1)S(1)}, u32[]{:S(2)}, u32[]{:S(2)}) collective-permute-start(bf16[128,5120]{1,0:T(8,128)(2,1)} %collective-permute-done.1), channel_id=1, source_target_pairs={{1,0},{2,1},{3,2},{5,4},{6,5},{7,6},{9,8},{10,9},{11,10},{13,12},{... | collective-permute-start | bytes 3932168 | tf_op jit(solution)/shard_map/ppermute | solution.py:95
  161.1 15.0 %copy-start.4 = (bf16[128,5120]{1,0:T(8,128)(2,1)}, bf16[128,5120]{1,0:T(8,128)(2,1)S(1)}, u32[]{:S(2)}) copy-start(bf16[128,5120]{1,0:T(8,128)(2,1)S(1)} %collective-permute-done.7) | copy-start | bytes 3932164
  161.1 20.8 %collective-permute-start.25 = (bf16[320,1536]{1,0:T(8,128)(2,1)S(1)}, bf16[320,1536]{1,0:T(8,128)(2,1)S(1)}, u32[]{:S(2)}, u32[]{:S(2)}) collective-permute-start(bf16[320,1536]{1,0:T(8,128)(2,1)S(1)} %collective-permute-done.23), channel_id=1, source_target_pairs={{0,4},{4,0},{8,12},{12,8},{1,5},{5,1},{9,13},{13,9},{2,6},{6,2},{1... | collective-permute-start | bytes 2949128 | tf_op jit(solution)/shard_map/ppermute | solution.py:72
  165.2 52.2 %copy-start.6 = (bf16[128,5120]{1,0:T(8,128)(2,1)}, bf16[128,5120]{1,0:T(8,128)(2,1)S(1)}, u32[]{:S(2)}) copy-start(bf16[128,5120]{1,0:T(8,128)(2,1)S(1)} %collective-permute-done.6) | copy-start | bytes 3932164
  165.2 33.9 %collective-permute-start.4 = (bf16[128,5120]{1,0:T(8,128)(2,1)}, bf16[128,5120]{1,0:T(8,128)(2,1)}, u32[]{:S(2)}, u32[]{:S(2)}) collective-permute-start(bf16[128,5120]{1,0:T(8,128)(2,1)} %collective-permute-done), channel_id=1, source_target_pairs={{0,1},{1,2},{2,3},{4,5},{5,6},{6,7},{8,9},{9,10},{10,11},{12,13},{... | collective-permute-start | bytes 3932168 | tf_op jit(solution)/shard_map/ppermute | solution.py:94
  176.1 41.3 %collective-permute-start.8 = (bf16[128,5120]{1,0:T(8,128)(2,1)S(1)}, bf16[128,5120]{1,0:T(8,128)(2,1)S(1)}, u32[]{:S(2)}, u32[]{:S(2)}) collective-permute-start(bf16[128,5120]{1,0:T(8,128)(2,1)S(1)} %collective-permute-done.7), channel_id=1, source_target_pairs={{1,0},{2,1},{3,2},{5,4},{6,5},{7,6},{9,8},{10,9},{11,10},{13,12},{... | collective-permute-start | bytes 3932168 | tf_op jit(solution)/shard_map/ppermute | solution.py:95
  178.6 48.6 %collective-permute-start.10 = (bf16[128,5120]{1,0:T(8,128)(2,1)S(1)}, bf16[128,5120]{1,0:T(8,128)(2,1)}, u32[]{:S(2)}, u32[]{:S(2)}) collective-permute-start(bf16[128,5120]{1,0:T(8,128)(2,1)S(1)} %collective-permute-done.6), channel_id=1, source_target_pairs={{0,1},{1,2},{2,3},{4,5},{5,6},{6,7},{8,9},{9,10},{10,11},{12,13},{... | collective-permute-start | bytes 3932168 | tf_op jit(solution)/shard_map/ppermute | solution.py:94
  181.9 47.6 %collective-permute-start.26 = (bf16[320,1536]{1,0:T(8,128)(2,1)S(1)}, bf16[320,1536]{1,0:T(8,128)(2,1)S(1)}, u32[]{:S(2)}, u32[]{:S(2)}) collective-permute-start(bf16[320,1536]{1,0:T(8,128)(2,1)S(1)} %collective-permute-done.24), channel_id=1, source_target_pairs={{0,4},{4,0},{8,12},{12,8},{1,5},{5,1},{9,13},{13,9},{2,6},{6,2},{1... | collective-permute-start | bytes 2949128 | tf_op jit(solution)/shard_map/ppermute | solution.py:72
  189.4 61.8 %collective-permute-start.3 = (bf16[128,5120]{1,0:T(8,128)(2,1)S(1)}, bf16[128,5120]{1,0:T(8,128)(2,1)}, u32[]{:S(2)}, u32[]{:S(2)}) collective-permute-start(bf16[128,5120]{1,0:T(8,128)(2,1)S(1)} %collective-permute-done.2), channel_id=1, source_target_pairs={{1,0},{2,1},{3,2},{5,4},{6,5},{7,6},{9,8},{10,9},{11,10},{13,12},{... | collective-permute-start | bytes 3932168 | tf_op jit(solution)/shard_map/ppermute | solution.py:95
  199.1 57.8 %collective-permute-start.5 = (bf16[128,5120]{1,0:T(8,128)(2,1)}, bf16[128,5120]{1,0:T(8,128)(2,1)}, u32[]{:S(2)}, u32[]{:S(2)}) collective-permute-start(bf16[128,5120]{1,0:T(8,128)(2,1)} %collective-permute-done.4), channel_id=1, source_target_pairs={{0,1},{1,2},{2,3},{4,5},{5,6},{6,7},{8,9},{9,10},{10,11},{12,13},{... | collective-permute-start | bytes 3932168 | tf_op jit(solution)/shard_map/ppermute | solution.py:94
  217.4 55.8 %collective-permute-start.9 = (bf16[128,5120]{1,0:T(8,128)(2,1)S(1)}, bf16[128,5120]{1,0:T(8,128)(2,1)}, u32[]{:S(2)}, u32[]{:S(2)}) collective-permute-start(bf16[128,5120]{1,0:T(8,128)(2,1)S(1)} %collective-permute-done.8), channel_id=1, source_target_pairs={{1,0},{2,1},{3,2},{5,4},{6,5},{7,6},{9,8},{10,9},{11,10},{13,12},{... | collective-permute-start | bytes 3932168 | tf_op jit(solution)/shard_map/ppermute | solution.py:95
  227.2 53.7 %collective-permute-start.11 = (bf16[128,5120]{1,0:T(8,128)(2,1)}, bf16[128,5120]{1,0:T(8,128)(2,1)}, u32[]{:S(2)}, u32[]{:S(2)}) collective-permute-start(bf16[128,5120]{1,0:T(8,128)(2,1)} %collective-permute-done.10), channel_id=1, source_target_pairs={{0,1},{1,2},{2,3},{4,5},{5,6},{6,7},{8,9},{9,10},{10,11},{12,13},{... | collective-permute-start | bytes 3932168 | tf_op jit(solution)/shard_map/ppermute | solution.py:94
  251.2 22.0 %copy-start.7 = (bf16[128,5120]{1,0:T(8,128)(2,1)S(1)}, bf16[128,5120]{1,0:T(8,128)(2,1)}, u32[]{:S(2)}) copy-start(bf16[128,5120]{1,0:T(8,128)(2,1)} %copy-done.6) | copy-start | bytes 3932164
  251.2 29.6 %copy-start.5 = (bf16[128,5120]{1,0:T(8,128)(2,1)S(1)}, bf16[128,5120]{1,0:T(8,128)(2,1)}, u32[]{:S(2)}) copy-start(bf16[128,5120]{1,0:T(8,128)(2,1)} %copy-done.4) | copy-start | bytes 3932164
  254.1 29.5 %copy-start.1 = (bf16[1536,5120]{1,0:T(8,128)(2,1)S(1)}, bf16[1536,5120]{1,0:T(8,128)(2,1)}, u32[]{:S(2)}) copy-start(bf16[1536,5120]{1,0:T(8,128)(2,1)} %copy.16) | copy-start | bytes 47185924
  283.5 24.3 %copy-start.11 = (f32[128]{0:T(128)S(1)}, f32[128]{0:T(128)}, u32[]{:S(2)}) copy-start(f32[128]{0:T(128)} %param.10) | copy-start | bytes 1540
  283.5 24.5 %copy-start.12 = (f32[128]{0:T(128)S(1)}, f32[128]{0:T(128)}, u32[]{:S(2)}) copy-start(f32[128]{0:T(128)} %param.9) | copy-start | bytes 1540
  307.1 3.9 %copy-start = (f32[1024,2,6,128]{0,3,2,1:T(8,128)}, f32[1024,2,6,128]{0,3,2,1:T(8,128)S(1)}, u32[]{:S(2)}) copy-start(f32[1024,2,6,128]{0,3,2,1:T(8,128)S(1)} %fusion.25) | copy-start | bytes 18874372
  307.8 3.2 copy-start.8

commit v2 on v0

--- a/solution.py
+++ b/solution.py
@@ -47,17 +47,19 @@
     return out.reshape(rows, -1).astype(jnp.bfloat16)
 
 
-def per_device(tokens, w_qkv, norm_gain, q_gain, k_gain, lengths):
+def gather_weights(w_qkv):
     tensor_count = lax.axis_size("tensor")
     fsdp_count = lax.axis_size("fsdp")
     local_rows = w_qkv.shape[0]
     columns = w_qkv.shape[1] // tensor_count
-    gathered = lax.all_gather(w_qkv, "fsdp", axis=0, tiled=True)
-    moved = lax.all_to_all(gathered, "tensor", split_axis=1, concat_axis=0, tiled=True)
-    blocks = moved.reshape(tensor_count, fsdp_count, local_rows, columns)
-    weight_cols = jnp.transpose(blocks, (1, 0, 2, 3)).reshape(
-        fsdp_count * tensor_count * local_rows, columns
-    )
+    moved = lax.all_to_all(w_qkv, "tensor", split_axis=1, concat_axis=0, tiled=True)
+    whole = lax.all_gather(moved, "fsdp", axis=0, tiled=True)
+    return whole.reshape(fsdp_count * tensor_count * local_rows, columns)
+
+
+def per_device(tokens, w_qkv, norm_gain, q_gain, k_gain, lengths):
+    tensor_count = lax.axis_size("tensor")
+    weight_cols = gather_weights(w_qkv)
     normed = head_norm(tokens.astype(jnp.float32), norm_gain).astype(jnp.bfloat16)
     qkv = jnp.dot(
         lax.all_gather(normed, "tensor", axis=0, tiled=True),

time: 772 us -> 465 us (0.60)
  waiting for transfers between devices: 606 us -> 163 us
  blocking collectives: 0 us -> 194 us
  local copies, waits for them, and re-layouts: 77.4 us -> 16.8 us
  other arithmetic: 8.02 us -> 18.4 us
    all_to_all x1 -> x0, waiting for transfers between devices: 502 us -> none  [per_device(): lax.all_to_all(gathered, 'tensor', split_axis=1, concat_axis=0, tiled=True)]
    all_to_all x0 -> x1, blocking collectives: none -> 194 us  [gather_weights(): lax.all_to_all(w_qkv, 'tensor', split_axis=1, concat_axis=0, tiled=True)]
    all_gather x1, waiting for transfers between devices: 0.01 us -> 60.7 us  [per_device(): lax.all_gather(normed, 'tensor', axis=0, tiled=True)]
    dot_general x1 -> x0, local copies, waits for them, and re-layouts: 20.7 us -> none  [per_device(): jnp.dot(lax.all_gather(normed, 'tensor', axis=0, tiled=True), weight_cols...]
    all_gather x1 -> x0, local copies, waits for them, and re-layouts: 19.2 us -> none  [per_device(): gathered = lax.all_gather(w_qkv, 'fsdp', axis=0, tiled=True)]
    all_to_all x1, local copies, waits for them, and re-layouts: 20.6 us -> 2.47 us  [gather_weights(): lax.all_to_all(w_qkv, 'tensor', split_axis=1, concat_axis=0, tiled=True)]
    transpose x1 -> x0, local copies, waits for them, and re-layouts: 13.2 us -> none  [per_device(): jnp.transpose(blocks, (1, 0, 2, 3))]
  transfers between devices with their start and end apart: 3 -> 2, of which waited for: 2 -> 2; matrix products, arithmetic and copies ran while one was open for 8% -> 1% of each run, Pallas kernels for 0% -> 0%
where the time goes in v2:
time: 465 us; the launch traced here: 463 us
  blocking collectives  194 us (42%)
  waiting for transfers between devices  163 us (35%)
  matrix products  55.9 us (12%)
  other arithmetic  18.4 us (4%)
  local copies, waits for them, and re-layouts  16.8 us (4%)
  between operations  14.2 us (3%)
    all_to_all x1, blocking collectives, gather_weights(): lax.all_to_all(w_qkv, 'tensor', split_axis=1, concat_axis=0, tiled=True)  194 us
    all_gather x1, waiting for transfers between devices, gather_weights(): whole = lax.all_gather(moved, 'fsdp', axis=0, tiled=True)  103 us
    all_gather x1, waiting for transfers between devices, per_device(): lax.all_gather(normed, 'tensor', axis=0, tiled=True)  60.7 us
    dot_general x1, matrix products, per_device(): jnp.dot(lax.all_gather(normed, 'tensor', axis=0, tiled=True), weight_cols...  22.7 us
    sub x1, matrix products, attend(): weights = jnp.exp(scores - top)  20.9 us
    dot_general x1, matrix products, attend(): jnp.einsum('kgij,jkd->ikgd', probs, value, preferred_element_type=jnp.flo...  12.2 us
  transfers between devices with their start and end apart: 2, of which 2 were waited for; matrix products, arithmetic and copies ran while one was open for 1% of the time, Pallas kernels for 0%

profile of v2, /device:TPU:24, one launch (start us, length us, event | category | flops | bytes accessed | tf_op | source)
XLA Modules:
  0.0 462.9 jit_solution(13617718968059551761)
XLA Ops:
  6.5 0.0 copy-start.1
  6.5 0.0 all-gather.3.cloned.1.call-start
  6.5 2.5 fusion.6
  9.0 0.0 copy-done.1
  9.1 3.0 fusion.8
  12.0 0.0 all-gather.3.cloned.1.call-update
  12.1 0.0 all-gather.5.cloned.1.call-start
  12.1 2.5 copy.45
  14.6 194.4 %all_to_all.19 = bf16[320,4,1536]{2,0,1:T(8,128)(2,1)} all-to-all(bf16[320,4,1536]{2,0,1:T(8,128)(2,1)S(1)} %bitcast.46), channel_id=1, replica_groups=mesh['groups'=2,'fsdp'=4,'tensor'=4] {'tensor'}, dimensions={1} | all-to-all | bytes 7864320 | tf_op jit(solution)/shard_map/all_to_all | solution.py:55
  209.0 0.0 all-gather.5.cloned.1.call-update
  209.7 1.9 multiply_cosine_fusion
  211.6 1.4 fusion.9
  212.9 60.7 %all-gather.3.cloned.1.call-done = bf16[1024,5120]{1,0:T(8,128)(2,1)} async-done(((bf16[256,5120]{1,0:T(8,128)(2,1)}), bf16[1024,5120]{1,0:T(8,128)(2,1)}) %all-gather.3.cloned.1.call-update) | async-done | bytes 10485776 | tf_op jit(solution)/shard_map/all_gather | solution.py:65
  273.6 102.5 %all-gather.5.cloned.1.call-done = bf16[5120,1536]{1,0:T(8,128)(2,1)} async-done(((bf16[1280,1536]{1,0:T(8,128)(2,1)}), bf16[5120,1536]{1,0:T(8,128)(2,1)}) %all-gather.5.cloned.1.call-update) | async-done | bytes 15728656 | tf_op jit(solution)/shard_map/all_gather | solution.py:56
  376.1 22.7 %fusion.23 = f32[1024,1536]{0,1:T(8,128)} fusion(bf16[1024,5120]{1,0:T(8,128)(2,1)} %all-gather.3.cloned.1.call-done, bf16[5120,1536]{1,0:T(8,128)(2,1)} %all-gather.5.cloned.1.call-done), kind=kOutput, calls=%fused_computation.45 | convolution fusion | flops 16106127360 | bytes 32505856 | tf_op jit(solution)/shard_map/dot_general | solution.py:64
  398.8 1.3 slice.30
  400.1 4.7 %slice.33 = f32[1024,2,4,128]{0,3,2,1:T(8,128)} slice(f32[1024,2,6,128]{0,3,2,1:T(8,128)} %bitcast.48), slice={[0:1024], [0:2], [0:4], [0:128]} | slice | bytes 8388608 | tf_op jit(solution)/shard_map/slice | solution.py:33
  404.8 0.3 copy.36
  405.1 0.4 multiply_reduce_fusion.1
  405.5 5.4 %copy.37 = f32[1024,2,4,128]{3,0,2,1:T(8,128)} copy(f32[1024,2,4,128]{0,3,2,1:T(8,128)} %slice.33) | data formatting | bytes 8388608
  410.9 0.0 copy-start.2
  410.9 0.0 copy-start
  410.9 0.0 copy-start.3
  410.9 3.5 multiply_reduce_fusion
  414.5 0.0 copy-done.2
  414.5 0.3 multiply_multiply_fusion.1
  414.8 0.0 copy-done
  414.8 0.0 copy-done.3
  414.8 1.2 multiply_multiply_fusion
  416.1 1.5 subtract_convert_fusion.1
  417.5 2.8 subtract_convert_fusion
  420.3 20.9 %fusion.22 = (f32[2,4,1024]{2,1,0:T(4,128)S(1)}, f32[2,4,1024,1024]{2,3,1,0:T(8,128)}) fusion(pred[1024,1024]{0,1:T(8,128)(4,1)} %fusion.9, bf16[1024,2,4,64]{3,0,2,1:T(8,128)(2,1)} %get-tuple-element.6, bf16[1024,2,4,64]{3,0,2,1:T(8,128)(2,1)S(1)} %get-tuple-element.5, bf16[1024,2,1,64]{3,0,1,2:T(8,128)(2,1)} %get-tuple-element.8, ...), kind=kOutput, calls=%fused_computation.44 | convolution fusion | flops 2186281984 | bytes 37257216 | tf_op jit(solution)/shard_map/sub | solution.py:44
  441.3 12.2 %fusion.12 = bf16[2,128,4,1024]{3,1,2,0:T(8,128)(2,1)S(1)} fusion(f32[2,4,1024,1024]{2,3,1,0:T(8,128)} %get-tuple-element.12, f32[2,4,1024]{2,1,0:T(4,128)S(1)} %get-tuple-element.11, f32[1024,2,6,128]{0,3,2,1:T(8,128)} %bitcast.49), kind=kOutput, calls=%fused_computation.23 | convolution fusion | flops 2165309440 | bytes 36208640 | tf_op jit(solution)/shard_map/kgij,jkd->ikgd/dot_general | solution.py:46
  453.5 2.6 copy.31
  (6 shorter events, 0.1 us)
Async XLA Ops:
  6.5 2.5 copy-start.1
  6.5 267.1 %all-gather.3.cloned.1.call-start = ((), (), s32[]{:S(2)}) async-start(), calls=%async_computation.1 | async-start | bytes 13107200 | tf_op jit(solution)/shard_map/all_gather | solution.py:65
  12.1 364.1 %all-gather.5.cloned.1.call-start = ((), (), s32[]{:S(2)}) async-start(), calls=%async_computation.2 | async-start | bytes 19660800 | tf_op jit(solution)/shard_map/all_gather | solution.py:56
  410.9 3.5 copy-start.2
  410.9 3.9 copy-start
  410.9 3.9 copy-start.3
Sparse Core Ops, SparseCore 0:
  12.2 261.3 all-gather.2
  275.2 100.9 all-gather.4

commit v3 on v2

--- a/solution.py
+++ b/solution.py
@@ -1,11 +1,16 @@
+import functools
 import jax
 import jax.numpy as jnp
 from jax import lax
+from jax.experimental import pallas as pl
+from jax.experimental.pallas import tpu as pltpu
 from jax.sharding import PartitionSpec as P
 
 KV = 8
 HD = 128
 GQ = 4
+LOG2E = 1.4426950408889634
+VMEM_BYTES = 52 * 1024 * 1024
 
 
 def head_norm(vec, gain):
@@ -13,10 +18,15 @@
     return vec * scale * gain
 
 
+def angles(positions):
+    half = HD // 2
+    freqs = 1000000.0 ** (-2.0 * jnp.arange(half, dtype=jnp.float32) / HD)
+    return positions.astype(jnp.float32)[:, None] * freqs[None, :]
+
+
 def rotate(vec, positions):
     half = vec.shape[-1] // 2
-    freqs = 1000000.0 ** (-2.0 * jnp.arange(half, dtype=jnp.float32) / vec.shape[-1])
-    angle = positions.astype(jnp.float32)[:, None] * freqs[None, :]
+    angle = angles(positions)
     cosine = jnp.cos(angle)[:, None, None, :]
     sine = jnp.sin(angle)[:, None, None, :]
     first = vec[..., :half]
@@ -47,28 +57,275 @@
     return out.reshape(rows, -1).astype(jnp.bfloat16)
 
 
-def gather_weights(w_qkv):
+def any_mesh(tokens, w_qkv, norm_gain, q_gain, k_gain, lengths):
     tensor_count = lax.axis_size("tensor")
-    fsdp_count = lax.axis_size("fsdp")
-    local_rows = w_qkv.shape[0]
-    columns = w_qkv.shape[1] // tensor_count
     moved = lax.all_to_all(w_qkv, "tensor", split_axis=1, concat_axis=0, tiled=True)
-    whole = lax.all_gather(moved, "fsdp", axis=0, tiled=True)
-    return whole.reshape(fsdp_count * tensor_count * local_rows, columns)
-
-
-def per_device(tokens, w_qkv, norm_gain, q_gain, k_gain, lengths):
-    tensor_count = lax.axis_size("tensor")
-    weight_cols = gather_weights(w_qkv)
+    weight_cols = lax.all_gather(moved, "fsdp", axis=0, tiled=True)
     normed = head_norm(tokens.astype(jnp.float32), norm_gain).astype(jnp.bfloat16)
     qkv = jnp.dot(
         lax.all_gather(normed, "tensor", axis=0, tiled=True),
         weight_cols,
         preferred_element_type=jnp.float32,
     )
-    kv_local = KV // tensor_count
-    qkv = qkv.reshape(qkv.shape[0], kv_local, GQ + 2, HD)
+    qkv = qkv.reshape(qkv.shape[0], KV // tensor_count, GQ + 2, HD)
     return attend(qkv, q_gain, k_gain, lengths[0])
+
+
+def project_kernel(blocks, tile, scal, *refs):
+    rows_refs = refs[:blocks]
+    pieces = refs[blocks : blocks + 16]
+    cos_ref, sin_ref, gain_ref = refs[blocks + 16 : blocks + 19]
+    outs = refs[blocks + 19 : 2 * blocks + 19]
+    held, total, sems = refs[2 * blocks + 19 :]
+    depth, columns = pieces[0].shape
+    band = 4 * depth
+
+    def copy(index):
+        group, slot = divmod(index, 4)
+        start = pl.multiple_of(scal[slot] * depth, 16)
+        return pltpu.make_async_copy(
+            pieces[index], held.at[group, pl.ds(start, depth), :], sems.at[index]
+        )
+
+    for index in range(16):
+        copy(index).start()
+    for group in range(4):
+        for slot in range(4):
+            copy(4 * group + slot).wait()
+        offset = pl.multiple_of(scal[4 + group] * band, 128)
+        first = 0
+        for ref in rows_refs:
+            rows = ref.shape[0]
+
+            @pl.loop(0, columns // tile)
+            def _(step, ref=ref, first=first, rows=rows):
+                at = pl.ds(pl.multiple_of(step * tile, tile), tile)
+                part = jnp.dot(
+                    ref[:, pl.ds(offset, band)],
+                    held[group, :, at],
+                    preferred_element_type=jnp.float32,
+                )
+                if group:
+                    part = part + total[first : first + rows, at]
+                total[first : first + rows, at] = part
+
+            first += rows
+    first = 0
+    for number, (ref, out) in enumerate(zip(rows_refs, outs)):
+        rows = ref.shape[0]
+        place = pl.ds(pl.multiple_of(scal[8 + number], 128), rows)
+        cosine = cos_ref[place, :]
+        sine = sin_ref[place, :]
+        for head in range(columns // HD):
+            kind = head % (GQ + 2)
+            at = slice(head * HD, (head + 1) * HD)
+            vec = total[first : first + rows, at]
+            if kind <= GQ:
+                scale = lax.rsqrt(jnp.mean(vec * vec, axis=-1, keepdims=True) + 1e-06)
+                gain = gain_ref[0:1, :] if kind < GQ else gain_ref[1:2, :]
+                vec = vec * scale * gain
+                vec = vec * cosine + pltpu.roll(vec, HD // 2, 1) * sine
+            out[:, at] = vec.astype(out.dtype)
+        first += rows
+
+
+def project(rows_list, places, pieces, scal, cos, sin, gains):
+    blocks = len(rows_list)
+    columns = pieces[0].shape[1]
+    depth = pieces[0].shape[0]
+    count = sum(r.shape[0] for r in rows_list)
+    width = rows_list[0].shape[1]
+    scal = jnp.concatenate([scal, jnp.stack(places)]).astype(jnp.int32)
+    vmem = pl.BlockSpec(memory_space=pltpu.VMEM)
+    return pl.pallas_call(
+        functools.partial(project_kernel, blocks, 512),
+        out_shape=[jax.ShapeDtypeStruct((r.shape[0], columns), jnp.bfloat16) for r in rows_list],
+        in_specs=[pl.BlockSpec(memory_space=pltpu.SMEM)]
+        + [vmem] * blocks
+        + [pl.BlockSpec(memory_space=pl.ANY)] * 16
+        + [vmem] * 3,
+        out_specs=[vmem] * blocks,
+        scratch_shapes=[
+            pltpu.VMEM((4, 4 * depth, columns), jnp.bfloat16),
+            pltpu.VMEM((count, columns), jnp.float32),
+            pltpu.SemaphoreType.DMA((16,)),
+        ],
+        compiler_params=pltpu.CompilerParams(vmem_limit_bytes=VMEM_BYTES),
+        cost_estimate=pl.CostEstimate(
+            flops=2 * count * width * columns,
+            bytes_accessed=2 * (width * columns + count * (width + columns)),
+            transcendentals=0,
+        ),
+        name="project",
+    )(scal, *rows_list, *pieces, cos, sin, gains)
+
+
+def attend_kernel(parts, block, scal, *refs):
+    near = refs[:parts]
+    far = refs[parts : 2 * parts]
+    out = refs[2 * parts]
+    held, sems = refs[2 * parts + 1 :]
+    middle = scal[0]
+    length = scal[1]
+    copies = []
+    for number in range(parts):
+        rows = near[number].shape[0]
+        place = pl.ds(pl.multiple_of(scal[2 + number], 128), rows)
+        copies.append(
+            [
+                pltpu.make_async_copy(ref, held.at[place, :], sems.at[number])
+                for ref in (near[number], far[number])
+            ]
+        )
+        pl.when(middle == 1)(copies[-1][0].start)
+        pl.when(middle == 0)(copies[-1][1].start)
+    for pair in copies:
+        pair[0].wait()
+    total = held.shape[0]
+    heads = held.shape[1] // ((GQ + 2) * HD)
+    factor = LOG2E / float(HD) ** 0.5
+    row = lax.broadcasted_iota(jnp.int32, (block, block), 0)
+    col = lax.broadcasted_iota(jnp.int32, (block, block), 1)
+    contract = (((1,), (1,)), ((), ()))
+    for group in range(heads):
+        base = group * (GQ + 2) * HD
+        key_at = slice(base + GQ * HD, base + (GQ + 1) * HD)
+        value_at = slice(base + (GQ + 1) * HD, base + (GQ + 2) * HD)
+
+        @pl.loop(0, GQ)
+        def _(j, base=base, key_at=key_at, value_at=value_at, group=group):
+            query_at = pl.ds(pl.multiple_of(base + j * HD, HD), HD)
+            out_at = pl.ds(pl.multiple_of((group * GQ + j) * HD, HD), HD)
+            for step in range(total // block):
+                low = step * block
+                high = low + block
+                query = held[low:high, query_at]
+                last = lax.dot_general(
+                    query, held[low:high, key_at], contract, preferred_element_type=jnp.float32
+                )
+                last = jnp.where((col <= row) & (col + low < length), last, -1e30)
+                top = jnp.max(last, axis=-1, keepdims=True)
+                if step:
+                    rest = lax.dot_general(
+                        query, held[:low, key_at], contract, preferred_element_type=jnp.float32
+                    )
+                    keys = lax.broadcasted_iota(jnp.int32, (1, low), 1)
+                    rest = rest + jnp.where(keys < length, 0.0, -1e30)
+                    top = jnp.maximum(top, jnp.max(rest, axis=-1, keepdims=True))
+                shift = top * factor
+                probs = jnp.exp2(last * factor - shift)
+                norm = jnp.sum(probs, axis=-1, keepdims=True)
+                value = jnp.dot(
+                    probs.astype(jnp.bfloat16),
+                    held[low:high, value_at],
+                    preferred_element_type=jnp.float32,
+                )
+                if step:
+                    probs = jnp.exp2(rest * factor - shift)
+                    norm = norm + jnp.sum(probs, axis=-1, keepdims=True)
+                    value = value + jnp.dot(
+                        probs.astype(jnp.bfloat16),
+                        held[:low, value_at],
+                        preferred_element_type=jnp.float32,
+                    )
+                out[low:high, out_at] = (value / norm).astype(out.dtype)
+
+
+def attend_blocks(near, far, places, middle, length):
+    parts = len(near)
+    rows = sum(n.shape[0] for n in near)
+    columns = near[0].shape[1]
+    wide = columns // (GQ + 2) * GQ
+    scal = jnp.stack([middle, length] + list(places)).astype(jnp.int32)
+    return pl.pallas_call(
+        functools.partial(attend_kernel, parts, 256),
+        out_shape=jax.ShapeDtypeStruct((rows, wide), jnp.bfloat16),
+        in_specs=[pl.BlockSpec(memory_space=pltpu.SMEM)]
+        + [pl.BlockSpec(memory_space=pl.ANY)] * (2 * parts),
+        out_specs=pl.BlockSpec(memory_space=pltpu.VMEM),
+        scratch_shapes=[
+            pltpu.VMEM((rows, columns), jnp.bfloat16),
+            pltpu.SemaphoreType.DMA((parts,)),
+        ],
+        compiler_params=pltpu.CompilerParams(vmem_limit_bytes=VMEM_BYTES),
+        cost_estimate=pl.CostEstimate(
+            flops=4 * rows * rows * wide,
+            bytes_accessed=2 * rows * (columns + wide),
+            transcendentals=rows * rows * wide // HD // 2,
+        ),
+        name="attend",
+    )(scal, *near, *far)
+
+
+def four_planes(tokens, w_qkv, norm_gain, q_gain, k_gain, lengths):
+    t = lax.axis_index("tensor")
+    f = lax.axis_index("fsdp")
+    rows = tokens.shape[0]
+    columns = w_qkv.shape[1] // 4
+    side = t // 2
+    end = 3 * side
+    mid = 1 + side
+    far_end = 3 * (1 - side)
+    far_mid = 2 - side
+
+    def slab(block):
+        return lax.dynamic_slice(w_qkv, (0, block * columns), (w_qkv.shape[0], columns))
+
+    def across(x, pairs):
+        return lax.ppermute(x, "tensor", pairs)
+
+    def beside(x, bit):
+        return lax.ppermute(x, "fsdp", [(i, i ^ bit) for i in range(4)])
+
+    inward = [(0, 1), (3, 2)]
+    swap = [(1, 2), (2, 1)]
+    far = [(0, 2), (3, 1)]
+    outward = [(1, 0), (2, 3)]
+
+    def collect(same, other):
+        mine = [same, across(same, inward), across(other, swap), across(other, far)]
+        over = [beside(x, 2) for x in mine]
+        return mine + over + [beside(x, 1) for x in mine] + [beside(x, 1) for x in over]
+
+    end_pieces = collect(slab(end), slab(far_end))
+    mid_pieces = collect(slab(mid), slab(far_mid))
+    scal = jnp.stack([mid, end, far_mid, far_end] + [jnp.bitwise_xor(f, m) for m in (0, 2, 1, 3)])
+
+    normed = head_norm(tokens.astype(jnp.float32), norm_gain).astype(jnp.bfloat16)
+    half = rows // 2
+    near_rows = [across(normed[:half], inward), across(normed[half:], inward)]
+    swap_rows = across(normed, swap)
+    far_rows = [across(x, swap) for x in near_rows]
+
+    positions = jnp.arange(4 * rows, dtype=jnp.int32)
+    angle = angles(positions)
+    cos = jnp.concatenate([jnp.cos(angle)] * 2, axis=1)
+    sin = jnp.concatenate([-jnp.sin(angle), jnp.sin(angle)], axis=1)
+    gains = jnp.stack([q_gain, k_gain])
+
+    blocks = [normed, swap_rows, near_rows[0], near_rows[1], far_rows[0], far_rows[1]]
+    places = [
+        mid * rows,
+        far_mid * rows,
+        end * rows,
+        end * rows + half,
+        far_end * rows,
+        far_end * rows + half,
+    ]
+
+    def run(picked, pieces):
+        return project(
+            [blocks[i] for i in picked], [places[i] for i in picked], pieces, scal, cos, sin, gains
+        )
+
+    sent = []
+    for picked in ([0], [1], [2, 3], [4], [5]):
+        sent += [across(x, outward) for x in run(picked, end_pieces)]
+    near = []
+    for picked in ([0, 1, 2, 3], [4], [5]):
+        near += run(picked, mid_pieces)
+    middle = jnp.where((t == 1) | (t == 2), 1, 0)
+    return attend_blocks(near, sent, places, middle, lengths[0])
 
 
 def solution(mesh):
@@ -80,8 +337,10 @@
         P(),
         P(("groups", "fsdp")),
     )
+    sizes = dict(mesh.shape)
+    body = four_planes if sizes["tensor"] == 4 and sizes["fsdp"] == 4 else any_mesh
     return jax.shard_map(
-        per_device,
+        body,
         mesh=mesh,
         in_specs=placed,
         out_specs=P(("groups", "fsdp"), "tensor"),

time: 465 us -> 434 us (0.933)
  blocking collectives: 194 us -> 0 us
  Pallas kernels: 0 us -> 125 us
  waiting for transfers between devices: 163 us -> 241 us
  matrix products: 55.9 us -> 0 us
  starting transfers between devices: 0.04 us -> 50.7 us
  other arithmetic: 18.4 us -> 5.1 us
  between operations: 14.2 us -> 1.52 us
  local copies, waits for them, and re-layouts: 16.8 us -> 7.67 us
    ppermute x0 -> x41, waiting for transfers between devices: none -> 241 us  [the longest x17 164 us: across(): return lax.ppermute(x, 'tensor', pairs)]
    all_to_all x1 -> x0, blocking collectives: 194 us -> none  [gather_weights(): lax.all_to_all(w_qkv, 'tensor', split_axis=1, concat_axis=0, tiled=True)]
    all_gather x2 -> x0, waiting for transfers between devices: 163 us -> none  [the longest x1 103 us: gather_weights(): whole = lax.all_gather(moved, 'fsdp', axis=0, tiled=True)]
    pallas_call x0 -> x9, Pallas kernels: none -> 125 us  [the longest x8 107 us: project(): pl.pallas_call(functools.partial(project_kernel, blocks, 512), out_shape=...]
    ppermute x0 -> x41, starting transfers between devices: none -> 50.7 us  [the longest x17 37.2 us: across(): return lax.ppermute(x, 'tensor', pairs)]
    dot_general x2 -> x0, matrix products: 34.9 us -> none  [the longest x1 22.7 us: per_device(): jnp.dot(lax.all_gather(normed, 'tensor', axis=0, tiled=True), weight_cols...]
    sub x1 -> x0, matrix products: 20.9 us -> none  [attend(): weights = jnp.exp(scores - top)]
    reduce_sum x3 -> x1, other arithmetic: 6.34 us -> 0.6 us  [head_norm(): scale = lax.rsqrt(jnp.mean(vec * vec, axis=-1, keepdims=True) + 1e-06)]
  transfers between devices with their start and end apart: 2 -> 41, of which waited for: 2 -> 14; matrix products, arithmetic and copies ran while one was open for 1% -> 2% of each run, Pallas kernels for 0% -> 25%
where the time goes in v3:
time: 434 us; the launch traced here: 431 us
  waiting for transfers between devices  241 us (56%)
  Pallas kernels  125 us (29%)
  starting transfers between devices  50.7 us (12%)
  local copies, waits for them, and re-layouts  7.67 us (2%)
  other arithmetic  5.1 us (1%)
    ppermute x17, waiting for transfers between devices, across(): return lax.ppermute(x, 'tensor', pairs)  164 us
    pallas_call x8, Pallas kernels, project(): pl.pallas_call(functools.partial(project_kernel, blocks, 512), out_shape=...  107 us
    ppermute x24, waiting for transfers between devices, beside(): return lax.ppermute(x, 'fsdp', [(i, i ^ bit) for i in range(4)])  77.8 us
    ppermute x17, starting transfers between devices, across(): return lax.ppermute(x, 'tensor', pairs)  37.2 us
    pallas_call x1, Pallas kernels, attend_blocks(): pl.pallas_call(functools.partial(attend_kernel, parts, 256), out_shape=ja...  17.6 us
    ppermute x24, starting transfers between devices, beside(): return lax.ppermute(x, 'fsdp', [(i, i ^ bit) for i in range(4)])  13.5 us
  transfers between devices with their start and end apart: 41, of which 14 were waited for; matrix products, arithmetic and copies ran while one was open for 2% of the time, Pallas kernels for 25%

profile of v3, /device:TPU:24, one launch (start us, length us, event | category | flops | bytes accessed | tf_op | source)
XLA Modules:
  0.0 431.1 jit_solution(8992184919329830750)
XLA Ops:
  0.0 2.5 constant_dynamic-slice_fusion
  2.5 0.9 collective-permute-start.4
  3.4 5.1 %collective-permute-start.5 = (bf16[320,1536]{1,0:T(8,128)(2,1)S(1)}, bf16[320,1536]{1,0:T(8,128)(2,1)S(1)}, u32[]{:S(2)}, u32[]{:S(2)}) collective-permute-start(bf16[320,1536]{1,0:T(8,128)(2,1)S(1)} %get-tuple-element.18), channel_id=1, source_target_pairs={{0,2},{3,1},{4,6},{7,5},{8,10},{11,9},{12,14},{15,13},{16,18},{19,... | collective-permute-start | bytes 2949128 | tf_op jit(solution)/shard_map/ppermute | solution.py:275
  8.5 1.4 collective-permute-start.3
  9.8 1.6 collective-permute-start.6
  11.4 0.6 fusion
  12.0 2.2 fusion.2.refs_0_
  14.3 36.0 %collective-permute-done.3.refs_5_.refs_2_ = bf16[320,1536]{1,0:T(8,128)(2,1)S(1)} collective-permute-done((bf16[320,1536]{1,0:T(8,128)(2,1)S(1)}, bf16[320,1536]{1,0:T(8,128)(2,1)S(1)}, u32[]{:S(2)}, u32[]{:S(2)}) %collective-permute-start.3) | collective-permute-done | bytes 983072 | tf_op jit(solution)/shard_map/ppermute | solution.py:275
  50.2 0.7 collective-permute-start.21
  51.0 7.1 %collective-permute-start.22 = (bf16[320,1536]{1,0:T(8,128)(2,1)S(1)}, bf16[320,1536]{1,0:T(8,128)(2,1)S(1)}, u32[]{:S(2)}, u32[]{:S(2)}) collective-permute-start(bf16[320,1536]{1,0:T(8,128)(2,1)S(1)} %get-tuple-element.17), channel_id=1, source_target_pairs={{0,2},{3,1},{4,6},{7,5},{8,10},{11,9},{12,14},{15,13},{16,18},{19,... | collective-permute-start | bytes 2949128 | tf_op jit(solution)/shard_map/ppermute | solution.py:275
  58.1 1.5 collective-permute-start.20
  59.6 1.9 fusion.4
  61.5 2.4 collective-permute-start.1
  63.9 1.5 collective-permute-start.23
  65.4 35.9 %collective-permute-done.20.refs_2_.refs_3_ = bf16[320,1536]{1,0:T(8,128)(2,1)S(1)} collective-permute-done((bf16[320,1536]{1,0:T(8,128)(2,1)S(1)}, bf16[320,1536]{1,0:T(8,128)(2,1)S(1)}, u32[]{:S(2)}, u32[]{:S(2)}) %collective-permute-start.20) | collective-permute-done | bytes 983072 | tf_op jit(solution)/shard_map/ppermute | solution.py:275
  101.3 5.5 %collective-permute-start.2 = (bf16[128,5120]{1,0:T(8,128)(2,1)S(1)}, bf16[128,5120]{1,0:T(8,128)(2,1)}, u32[]{:S(2)}, u32[]{:S(2)}) collective-permute-start(bf16[128,5120]{1,0:T(8,128)(2,1)S(1)} %get-tuple-element.21), channel_id=1, source_target_pairs={{0,1},{3,2},{4,5},{7,6},{8,9},{11,10},{12,13},{15,14},{16,17},{19,... | collective-permute-start | bytes 3932168 | tf_op jit(solution)/shard_map/ppermute | solution.py:275
  106.9 1.6 collective-permute-start.7
  108.4 0.6 collective-permute-start.8
  109.0 0.4 collective-permute-done.27.refs_9_.refs_10_
  109.4 1.5 collective-permute-start.9
  110.9 18.5 %collective-permute-done.1.refs_2_.refs_0_ = bf16[128,5120]{1,0:T(8,128)(2,1)} collective-permute-done((bf16[128,5120]{1,0:T(8,128)(2,1)S(1)}, bf16[128,5120]{1,0:T(8,128)(2,1)}, u32[]{:S(2)}, u32[]{:S(2)}) %collective-permute-start.1) | collective-permute-done | bytes 1310752 | tf_op jit(solution)/shard_map/ppermute | solution.py:275
  129.4 25.5 %collective-permute-done.2.refs_3_.refs_1_ = bf16[128,5120]{1,0:T(8,128)(2,1)} collective-permute-done((bf16[128,5120]{1,0:T(8,128)(2,1)S(1)}, bf16[128,5120]{1,0:T(8,128)(2,1)}, u32[]{:S(2)}, u32[]{:S(2)}) %collective-permute-start.2) | collective-permute-done | bytes 1310752 | tf_op jit(solution)/shard_map/ppermute | solution.py:275
  154.9 1.5 collective-permute-start.24
  156.4 0.5 collective-permute-start.25
  156.9 1.5 collective-permute-start.26
  158.4 15.3 %collective-permute-done.9.refs_11_.refs_8_ = bf16[320,1536]{1,0:T(8,128)(2,1)} collective-permute-done((bf16[320,1536]{1,0:T(8,128)(2,1)S(1)}, bf16[320,1536]{1,0:T(8,128)(2,1)}, u32[]{:S(2)}, u32[]{:S(2)}) %collective-permute-start.9) | collective-permute-done | bytes 983072 | tf_op jit(solution)/shard_map/ppermute | solution.py:278
  173.7 0.5 collective-permute-start.29
  174.2 20.4 %collective-permute-done.24.refs_6_.refs_7_ = bf16[320,1536]{1,0:T(8,128)(2,1)S(1)} collective-permute-done((bf16[320,1536]{1,0:T(8,128)(2,1)S(1)}, bf16[320,1536]{1,0:T(8,128)(2,1)S(1)}, u32[]{:S(2)}, u32[]{:S(2)}) %collective-permute-start.24) | collective-permute-done | bytes 983072 | tf_op jit(solution)/shard_map/ppermute | solution.py:278
  194.7 21.2 %collective-permute-done.25.refs_7_.refs_8_ = bf16[320,1536]{1,0:T(8,128)(2,1)} collective-permute-done((bf16[320,1536]{1,0:T(8,128)(2,1)S(1)}, bf16[320,1536]{1,0:T(8,128)(2,1)}, u32[]{:S(2)}, u32[]{:S(2)}) %collective-permute-start.25) | collective-permute-done | bytes 983072 | tf_op jit(solution)/shard_map/ppermute | solution.py:278
  215.9 2.2 collective-permute-start
  218.0 18.4 %collective-permute-done.26.refs_8_.refs_9_ = bf16[320,1536]{1,0:T(8,128)(2,1)} collective-permute-done((bf16[320,1536]{1,0:T(8,128)(2,1)S(1)}, bf16[320,1536]{1,0:T(8,128)(2,1)}, u32[]{:S(2)}, u32[]{:S(2)}) %collective-permute-start.26) | collective-permute-done | bytes 983072 | tf_op jit(solution)/shard_map/ppermute | solution.py:278
  236.5 0.5 collective-permute-start.32
  237.1 0.5 collective-permute-start.34
  237.6 2.1 collective-permute-done.31.refs_13_.refs_14_
  239.7 0.9 copy-done.10
  240.7 1.7 collective-permute-start.18
  243.9 0.4 collective-permute-start.13
  244.3 0.9 collective-permute-start.19
  245.2 1.9 fusion.3
  247.1 0.3 pad_maximum_fusion
  247.5 11.8 %project.11 = bf16[256,1536]{1,0:T(8,128)(2,1)S(1)} custom-call(s32[9]{0:T(128)S(1)} %concatenate.39.scal, bf16[256,5120]{1,0:T(8,128)(2,1)} %fusion.2.refs_0_, bf16[320,1536]{1,0:T(8,128)(2,1)} %copy-done, bf16[320,1536]{1,0:T(8,128)(2,1)} %copy-done.3, bf16[320,1536]{1,0:T(8,128)(2,1)} %copy-done.1, bf16[320,1536]{1,0:T(8,128)(2,1)} %copy-done.2, ...), custom_call_target="tpu_custom_call" | custom-call | flops 4026531840 | bytes 19136512 | tf_op jit(solution)/shard_map/project/pallas_call | solution.py:140
  259.5 0.4 collective-permute-start.15
  260.3 0.2 collective-permute-start.17
  260.7 9.1 %project.14 = bf16[128,1536]{1,0:T(8,128)(2,1)S(1)} custom-call(s32[9]{0:T(128)S(1)} %concatenate.37.scal, bf16[128,5120]{1,0:T(8,128)(2,1)} %collective-permute-done.18.refs_0_, bf16[320,1536]{1,0:T(8,128)(2,1)} %copy-done, bf16[320,1536]{1,0:T(8,128)(2,1)} %copy-done.3, bf16[320,1536]{1,0:T(8,128)(2,1)} %copy-done.1, bf16[320,1536]{1,0:T(8,128)(2,1)} %copy-done.2, ...), custom_call_target="tpu_custom_call" | custom-call | flops 2013265920 | bytes 17432576 | tf_op jit(solution)/shard_map/project/pallas_call | solution.py:140
  269.8 14.7 %project.13 = (bf16[128,1536]{1,0:T(8,128)(2,1)S(1)}, bf16[128,1536]{1,0:T(8,128)(2,1)S(1)}) custom-call(s32[10]{0:T(128)S(1)} %concatenate.41.scal, bf16[128,5120]{1,0:T(8,128)(2,1)} %collective-permute-done.1.refs_2_.refs_0_, bf16[128,5120]{1,0:T(8,128)(2,1)} %collective-permute-done.2.refs_3_.refs_1_, bf16[320,1536]{1,0:T(8,128)(2,1)} %copy-done, ...), custom_call_target="tpu_custom_call" | custom-call | flops 4026531840 | bytes 19136512 | tf_op jit(solution)/shard_map/project/pallas_call | solution.py:140
  284.5 1.5 collective-permute-start.37
  286.0 9.1 %project.15 = bf16[128,1536]{1,0:T(8,128)(2,1)S(1)} custom-call(s32[9]{0:T(128)S(1)} %concatenate.38.scal, bf16[128,5120]{1,0:T(8,128)(2,1)} %copy-done.13, bf16[320,1536]{1,0:T(8,128)(2,1)} %copy-done, bf16[320,1536]{1,0:T(8,128)(2,1)} %copy-done.3, bf16[320,1536]{1,0:T(8,128)(2,1)} %copy-done.1, bf16[320,1536]{1,0:T(8,128)(2,1)} %copy-done.2, ...), custom_call_target="tpu_custom_call" | custom-call | flops 2013265920 | bytes 17432576 | tf_op jit(solution)/shard_map/project/pallas_call | solution.py:140
  295.1 11.6 %project.12 = bf16[256,1536]{1,0:T(8,128)(2,1)S(1)} custom-call(s32[9]{0:T(128)S(1)} %concatenate.40.scal, bf16[256,5120]{1,0:T(8,128)(2,1)} %collective-permute-done.refs_1_.refs_0_, bf16[320,1536]{1,0:T(8,128)(2,1)} %copy-done, bf16[320,1536]{1,0:T(8,128)(2,1)} %copy-done.3, bf16[320,1536]{1,0:T(8,128)(2,1)} %copy-done.1, bf16[320,1536]{1,0:T(8,128)(2,1)} %copy-done.2, ...), custom_call_target="tpu_custom_call" | custom-call | flops 4026531840 | bytes 19136512 | tf_op jit(solution)/shard_map/project/pallas_call | solution.py:140
  306.8 1.3 collective-permute-start.35
  308.1 1.3 collective-permute-start.36
  309.4 1.3 collective-permute-start.38
  310.7 1.3 collective-permute-start.39
  312.0 27.2 %collective-permute-done.37.refs_8_ = bf16[128,1536]{1,0:T(8,128)(2,1)S(1)} collective-permute-done((bf16[128,1536]{1,0:T(8,128)(2,1)S(1)}, bf16[128,1536]{1,0:T(8,128)(2,1)S(1)}, u32[]{:S(2)}, u32[]{:S(2)}) %collective-permute-start.37) | collective-permute-done | bytes 393248 | tf_op jit(solution)/shard_map/ppermute | solution.py:275
  339.2 1.3 collective-permute-start.40
  340.5 32.7 %project.8 = (bf16[256,1536]{1,0:T(8,128)(2,1)}, bf16[256,1536]{1,0:T(8,128)(2,1)}, bf16[128,1536]{1,0:T(8,128)(2,1)S(1)}, bf16[128,1536]{1,0:T(8,128)(2,1)S(1)}) custom-call(s32[12]{0:T(128)S(1)} %concatenate.34.scal, bf16[256,5120]{1,0:T(8,128)(2,1)} %fusion.2.refs_0_, bf16[256,5120]{1,0:T(8,128)(2,1)} %collective-permute-done.refs_1_.refs_0_, ...), custom_call_target="tpu_custom_call" | custom-call | flops 12079595520 | bytes 25952256 | tf_op jit(solution)/shard_map/project/pallas_call | solution.py:140
  373.2 9.1 %project.9.refs_4_ = bf16[128,1536]{1,0:T(8,128)(2,1)S(1)} custom-call(s32[9]{0:T(128)S(1)} %concatenate.37.scal, bf16[128,5120]{1,0:T(8,128)(2,1)} %collective-permute-done.18.refs_0_, bf16[320,1536]{1,0:T(8,128)(2,1)} %copy-done.12, bf16[320,1536]{1,0:T(8,128)(2,1)} %copy-done.16, bf16[320,1536]{1,0:T(8,128)(2,1)} %copy-done.14, ...), custom_call_target="tpu_custom_call" | custom-call | flops 2013265920 | bytes 17432576 | tf_op jit(solution)/shard_map/project/pallas_call | solution.py:140
  382.3 9.1 %project.10.refs_5_ = bf16[128,1536]{1,0:T(8,128)(2,1)S(1)} custom-call(s32[9]{0:T(128)S(1)} %concatenate.38.scal, bf16[128,5120]{1,0:T(8,128)(2,1)} %copy-done.13, bf16[320,1536]{1,0:T(8,128)(2,1)} %copy-done.12, bf16[320,1536]{1,0:T(8,128)(2,1)} %copy-done.16, bf16[320,1536]{1,0:T(8,128)(2,1)} %copy-done.14, bf16[320,1536]{1,0:T(8,128)(2,1)} %copy-done.15, ...), custom_call_target="tpu_custom_call" | custom-call | flops 2013265920 | bytes 17432576 | tf_op jit(solution)/shard_map/project/pallas_call | solution.py:140
  391.4 6.3 %collective-permute-done.38.refs_9_ = bf16[128,1536]{1,0:T(8,128)(2,1)S(1)} collective-permute-done((bf16[128,1536]{1,0:T(8,128)(2,1)S(1)}, bf16[128,1536]{1,0:T(8,128)(2,1)S(1)}, u32[]{:S(2)}, u32[]{:S(2)}) %collective-permute-start.38) | collective-permute-done | bytes 393248 | tf_op jit(solution)/shard_map/ppermute | solution.py:275
  397.7 8.4 %collective-permute-done.39.refs_10_ = bf16[128,1536]{1,0:T(8,128)(2,1)S(1)} collective-permute-done((bf16[128,1536]{1,0:T(8,128)(2,1)S(1)}, bf16[128,1536]{1,0:T(8,128)(2,1)S(1)}, u32[]{:S(2)}, u32[]{:S(2)}) %collective-permute-start.39) | collective-permute-done | bytes 393248 | tf_op jit(solution)/shard_map/ppermute | solution.py:275
  406.1 5.9 %collective-permute-done.40.refs_11_ = bf16[128,1536]{1,0:T(8,128)(2,1)S(1)} collective-permute-done((bf16[128,1536]{1,0:T(8,128)(2,1)S(1)}, bf16[128,1536]{1,0:T(8,128)(2,1)S(1)}, u32[]{:S(2)}, u32[]{:S(2)}) %collective-permute-start.40) | collective-permute-done | bytes 393248 | tf_op jit(solution)/shard_map/ppermute | solution.py:275
  412.0 0.7 copy-done.37
  412.8 0.3 copy-done.33
  413.1 0.3 copy-done.34
  413.3 17.6 %attend.1 = bf16[1024,1024]{1,0:T(8,128)(2,1)} custom-call(s32[8]{0:T(128)S(1)} %stack.77.scal, bf16[256,1536]{1,0:T(8,128)(2,1)} %get-tuple-element.11.refs_0_, bf16[256,1536]{1,0:T(8,128)(2,1)} %get-tuple-element.12.refs_1_, bf16[128,1536]{1,0:T(8,128)(2,1)S(1)} %get-tuple-element.13.refs_2_, bf16[128,1536]{1,0:T(8,128)(2,1)S(1)} %get-tuple-element.14.refs_3_, ...), custom_call_target="tpu_custom_call" | custom-call | flops 4294967296 | bytes 5242880 | tf_op jit(solution)/shard_map/attend/pallas_call | solution.py:240
  (120 shorter events, 1.8 us)
Async XLA Ops:
  2.5 104.3 %copy-start = (bf16[320,1536]{1,0:T(8,128)(2,1)}, bf16[320,1536]{1,0:T(8,128)(2,1)S(1)}, u32[]{:S(2)}) copy-start(bf16[320,1536]{1,0:T(8,128)(2,1)S(1)} %get-tuple-element.20.refs_1_.refs_2_) | copy-start | bytes 2949124
  2.5 48.4 %collective-permute-start.4 = (bf16[320,1536]{1,0:T(8,128)(2,1)S(1)}, bf16[320,1536]{1,0:T(8,128)(2,1)S(1)}, u32[]{:S(2)}, u32[]{:S(2)}) collective-permute-start(bf16[320,1536]{1,0:T(8,128)(2,1)S(1)} %get-tuple-element.18), channel_id=1, source_target_pairs={{1,2},{2,1},{5,6},{6,5},{9,10},{10,9},{13,14},{14,13},{17,18},{18,... | collective-permute-start | bytes 2949128 | tf_op jit(solution)/shard_map/ppermute | solution.py:275
  3.4 54.7 %collective-permute-start.5 = (bf16[320,1536]{1,0:T(8,128)(2,1)S(1)}, bf16[320,1536]{1,0:T(8,128)(2,1)S(1)}, u32[]{:S(2)}, u32[]{:S(2)}) collective-permute-start(bf16[320,1536]{1,0:T(8,128)(2,1)S(1)} %get-tuple-element.18), channel_id=1, source_target_pairs={{0,2},{3,1},{4,6},{7,5},{8,10},{11,9},{12,14},{15,13},{16,18},{19,... | collective-permute-start | bytes 2949128 | tf_op jit(solution)/shard_map/ppermute | solution.py:275
  8.5 41.8 %collective-permute-start.3 = (bf16[320,1536]{1,0:T(8,128)(2,1)S(1)}, bf16[320,1536]{1,0:T(8,128)(2,1)S(1)}, u32[]{:S(2)}, u32[]{:S(2)}) collective-permute-start(bf16[320,1536]{1,0:T(8,128)(2,1)S(1)} %get-tuple-element.19.refs_4_.refs_1_), channel_id=1, source_target_pairs={{0,1},{3,2},{4,5},{7,6},{8,9},{11,10},{12,13},{15,14},{16,17},{19,... | collective-permute-start | bytes 2949128 | tf_op jit(solution)/shard_map/ppermute | solution.py:275
  9.8 51.7 %collective-permute-start.6 = (bf16[320,1536]{1,0:T(8,128)(2,1)S(1)}, bf16[320,1536]{1,0:T(8,128)(2,1)S(1)}, u32[]{:S(2)}, u32[]{:S(2)}) collective-permute-start(bf16[320,1536]{1,0:T(8,128)(2,1)S(1)} %get-tuple-element.19.refs_4_.refs_1_), channel_id=1, source_target_pairs={{0,8},{4,12},{8,0},{12,4},{1,9},{5,13},{9,1},{13,5},{2,10},{6,14},... | collective-permute-start | bytes 2949128 | tf_op jit(solution)/shard_map/ppermute | solution.py:278
  11.4 52.5 %collective-permute-start.10 = (bf16[320,1536]{1,0:T(8,128)(2,1)S(1)}, bf16[320,1536]{1,0:T(8,128)(2,1)S(1)}, u32[]{:S(2)}, u32[]{:S(2)}) collective-permute-start(bf16[320,1536]{1,0:T(8,128)(2,1)S(1)} %get-tuple-element.19.refs_4_.refs_1_), channel_id=1, source_target_pairs={{0,4},{4,0},{8,12},{12,8},{1,5},{5,1},{9,13},{13,9},{2,6},{6,2},{1... | collective-permute-start | bytes 2949128 | tf_op jit(solution)/shard_map/ppermute | solution.py:278
  50.2 79.1 %copy-start.16 = (bf16[320,1536]{1,0:T(8,128)(2,1)}, bf16[320,1536]{1,0:T(8,128)(2,1)S(1)}, u32[]{:S(2)}) copy-start(bf16[320,1536]{1,0:T(8,128)(2,1)S(1)} %collective-permute-done.3.refs_5_.refs_2_) | copy-start | bytes 2949124
  50.2 56.6 %collective-permute-start.21 = (bf16[320,1536]{1,0:T(8,128)(2,1)S(1)}, bf16[320,1536]{1,0:T(8,128)(2,1)S(1)}, u32[]{:S(2)}, u32[]{:S(2)}) collective-permute-start(bf16[320,1536]{1,0:T(8,128)(2,1)S(1)} %get-tuple-element.17), channel_id=1, source_target_pairs={{1,2},{2,1},{5,6},{6,5},{9,10},{10,9},{13,14},{14,13},{17,18},{18,... | collective-permute-start | bytes 2949128 | tf_op jit(solution)/shard_map/ppermute | solution.py:275
  51.0 57.5 %copy-start.14 = (bf16[320,1536]{1,0:T(8,128)(2,1)}, bf16[320,1536]{1,0:T(8,128)(2,1)S(1)}, u32[]{:S(2)}) copy-start(bf16[320,1536]{1,0:T(8,128)(2,1)S(1)} %collective-permute-done.4.refs_6_.refs_3_) | copy-start | bytes 2949124
  51.0 55.9 %collective-permute-start.22 = (bf16[320,1536]{1,0:T(8,128)(2,1)S(1)}, bf16[320,1536]{1,0:T(8,128)(2,1)S(1)}, u32[]{:S(2)}, u32[]{:S(2)}) collective-permute-start(bf16[320,1536]{1,0:T(8,128)(2,1)S(1)} %get-tuple-element.17), channel_id=1, source_target_pairs={{0,2},{3,1},{4,6},{7,5},{8,10},{11,9},{12,14},{15,13},{16,18},{19,... | collective-permute-start | bytes 2949128 | tf_op jit(solution)/shard_map/ppermute | solution.py:275
  58.1 51.3 %copy-start.15 = (bf16[320,1536]{1,0:T(8,128)(2,1)}, bf16[320,1536]{1,0:T(8,128)(2,1)S(1)}, u32[]{:S(2)}) copy-start(bf16[320,1536]{1,0:T(8,128)(2,1)S(1)} %collective-permute-done.5.refs_7_.refs_4_) | copy-start | bytes 2949124
  58.1 185.5 %copy-start.31 = (f32[128]{0:T(128)S(1)}, f32[128]{0:T(128)}, u32[]{:S(2)}) copy-start(f32[128]{0:T(128)} %param.10) | copy-start | bytes 1540
  58.1 185.5 %copy-start.32 = (f32[128]{0:T(128)S(1)}, f32[128]{0:T(128)}, u32[]{:S(2)}) copy-start(f32[128]{0:T(128)} %param.9) | copy-start | bytes 1540
  58.1 43.2 %collective-permute-start.20 = (bf16[320,1536]{1,0:T(8,128)(2,1)S(1)}, bf16[320,1536]{1,0:T(8,128)(2,1)S(1)}, u32[]{:S(2)}, u32[]{:S(2)}) collective-permute-start(bf16[320,1536]{1,0:T(8,128)(2,1)S(1)} %get-tuple-element.20.refs_1_.refs_2_), channel_id=1, source_target_pairs={{0,1},{3,2},{4,5},{7,6},{8,9},{11,10},{12,13},{15,14},{16,17},{19,... | collective-permute-start | bytes 2949128 | tf_op jit(solution)/shard_map/ppermute | solution.py:275
  61.5 178.1 %copy-start.17 = (bf16[320,1536]{1,0:T(8,128)(2,1)}, bf16[320,1536]{1,0:T(8,128)(2,1)S(1)}, u32[]{:S(2)}) copy-start(bf16[320,1536]{1,0:T(8,128)(2,1)S(1)} %collective-permute-done.6.refs_8_.refs_5_) | copy-start | bytes 2949124
  61.5 67.8 %collective-permute-start.1 = (bf16[128,5120]{1,0:T(8,128)(2,1)S(1)}, bf16[128,5120]{1,0:T(8,128)(2,1)}, u32[]{:S(2)}, u32[]{:S(2)}) collective-permute-start(bf16[128,5120]{1,0:T(8,128)(2,1)S(1)} %get-tuple-element.22), channel_id=1, source_target_pairs={{0,1},{3,2},{4,5},{7,6},{8,9},{11,10},{12,13},{15,14},{16,17},{19,... | collective-permute-start | bytes 3932168 | tf_op jit(solution)/shard_map/ppermute | solution.py:275
  63.9 175.8 %copy-start.19 = (bf16[320,1536]{1,0:T(8,128)(2,1)}, bf16[320,1536]{1,0:T(8,128)(2,1)S(1)}, u32[]{:S(2)}) copy-start(bf16[320,1536]{1,0:T(8,128)(2,1)S(1)} %collective-permute-done.10.refs_12_.refs_9_) | copy-start | bytes 2949124
  63.9 44.6 %collective-permute-start.23 = (bf16[320,1536]{1,0:T(8,128)(2,1)S(1)}, bf16[320,1536]{1,0:T(8,128)(2,1)S(1)}, u32[]{:S(2)}, u32[]{:S(2)}) collective-permute-start(bf16[320,1536]{1,0:T(8,128)(2,1)S(1)} %get-tuple-element.20.refs_1_.refs_2_), channel_id=1, source_target_pairs={{0,8},{4,12},{8,0},{12,4},{1,9},{5,13},{9,1},{13,5},{2,10},{6,14},... | collective-permute-start | bytes 2949128 | tf_op jit(solution)/shard_map/ppermute | solution.py:278
  101.3 135.8 %copy-start.3 = (bf16[320,1536]{1,0:T(8,128)(2,1)}, bf16[320,1536]{1,0:T(8,128)(2,1)S(1)}, u32[]{:S(2)}) copy-start(bf16[320,1536]{1,0:T(8,128)(2,1)S(1)} %collective-permute-done.20.refs_2_.refs_3_) | copy-start | bytes 2949124
  101.3 53.6 %collective-permute-start.2 = (bf16[128,5120]{1,0:T(8,128)(2,1)S(1)}, bf16[128,5120]{1,0:T(8,128)(2,1)}, u32[]{:S(2)}, u32[]{:S(2)}) collective-permute-start(bf16[128,5120]{1,0:T(8,128)(2,1)S(1)} %get-tuple-element.21), channel_id=1, source_target_pairs={{0,1},{3,2},{4,5},{7,6},{8,9},{11,10},{12,13},{15,14},{16,17},{19,... | collective-permute-start | bytes 3932168 | tf_op jit(solution)/shard_map/ppermute | solution.py:275
  106.8 140.7 %copy-start.1 = (bf16[320,1536]{1,0:T(8,128)(2,1)}, bf16[320,1536]{1,0:T(8,128)(2,1)S(1)}, u32[]{:S(2)}) copy-start(bf16[320,1536]{1,0:T(8,128)(2,1)S(1)} %collective-permute-done.21.refs_3_.refs_4_) | copy-start | bytes 2949124
  106.8 2.6 collective-permute-start.27
  106.8 140.6 %copy-start.2 = (bf16[320,1536]{1,0:T(8,128)(2,1)}, bf16[320,1536]{1,0:T(8,128)(2,1)S(1)}, u32[]{:S(2)}) copy-start(bf16[320,1536]{1,0:T(8,128)(2,1)S(1)} %collective-permute-done.22.refs_4_.refs_5_) | copy-start | bytes 2949124
  106.9 49.5 %collective-permute-start.7 = (bf16[320,1536]{1,0:T(8,128)(2,1)S(1)}, bf16[320,1536]{1,0:T(8,128)(2,1)S(1)}, u32[]{:S(2)}, u32[]{:S(2)}) collective-permute-start(bf16[320,1536]{1,0:T(8,128)(2,1)S(1)} %collective-permute-done.3.refs_5_.refs_2_), channel_id=1, source_target_pairs={{0,8},{4,12},{8,0},{12,4},{1,9},{5,13},{9,1},{13,5},{2,10},{6,14},... | collective-permute-start | bytes 2949128 | tf_op jit(solution)/shard_map/ppermute | solution.py:278
  108.4 129.1 %copy-start.4 = (bf16[320,1536]{1,0:T(8,128)(2,1)}, bf16[320,1536]{1,0:T(8,128)(2,1)S(1)}, u32[]{:S(2)}) copy-start(bf16[320,1536]{1,0:T(8,128)(2,1)S(1)} %collective-permute-done.23.refs_5_.refs_6_) | copy-start | bytes 2949124
  108.4 48.5 %collective-permute-start.8 = (bf16[320,1536]{1,0:T(8,128)(2,1)S(1)}, bf16[320,1536]{1,0:T(8,128)(2,1)S(1)}, u32[]{:S(2)}, u32[]{:S(2)}) collective-permute-start(bf16[320,1536]{1,0:T(8,128)(2,1)S(1)} %collective-permute-done.4.refs_6_.refs_3_), channel_id=1, source_target_pairs={{0,8},{4,12},{8,0},{12,4},{1,9},{5,13},{9,1},{13,5},{2,10},{6,14},... | collective-permute-start | bytes 2949128 | tf_op jit(solution)/shard_map/ppermute | solution.py:278
  109.4 130.3 %copy-start.5 = (bf16[320,1536]{1,0:T(8,128)(2,1)}, bf16[320,1536]{1,0:T(8,128)(2,1)S(1)}, u32[]{:S(2)}) copy-start(bf16[320,1536]{1,0:T(8,128)(2,1)S(1)} %collective-permute-done.27.refs_9_.refs_10_) | copy-start | bytes 2949124
  109.4 64.3 %collective-permute-start.9 = (bf16[320,1536]{1,0:T(8,128)(2,1)S(1)}, bf16[320,1536]{1,0:T(8,128)(2,1)}, u32[]{:S(2)}, u32[]{:S(2)}) collective-permute-start(bf16[320,1536]{1,0:T(8,128)(2,1)S(1)} %collective-permute-done.5.refs_7_.refs_4_), channel_id=1, source_target_pairs={{0,8},{4,12},{8,0},{12,4},{1,9},{5,13},{9,1},{13,5},{2,10},{6,14},... | collective-permute-start | bytes 2949128 | tf_op jit(solution)/shard_map/ppermute | solution.py:278
  129.4 44.4 %collective-permute-start.11 = (bf16[320,1536]{1,0:T(8,128)(2,1)S(1)}, bf16[320,1536]{1,0:T(8,128)(2,1)S(1)}, u32[]{:S(2)}, u32[]{:S(2)}) collective-permute-start(bf16[320,1536]{1,0:T(8,128)(2,1)S(1)} %collective-permute-done.3.refs_5_.refs_2_), channel_id=1, source_target_pairs={{0,4},{4,0},{8,12},{12,8},{1,5},{5,1},{9,13},{13,9},{2,6},{6,2},{1... | collective-permute-start | bytes 2949128 | tf_op jit(solution)/shard_map/ppermute | solution.py:278
  154.9 39.8 %collective-permute-start.24 = (bf16[320,1536]{1,0:T(8,128)(2,1)S(1)}, bf16[320,1536]{1,0:T(8,128)(2,1)S(1)}, u32[]{:S(2)}, u32[]{:S(2)}) collective-permute-start(bf16[320,1536]{1,0:T(8,128)(2,1)S(1)} %collective-permute-done.20.refs_2_.refs_3_), channel_id=1, source_target_pairs={{0,8},{4,12},{8,0},{12,4},{1,9},{5,13},{9,1},{13,5},{2,10},{6,14},... | collective-permute-start | bytes 2949128 | tf_op jit(solution)/shard_map/ppermute | solution.py:278
  156.4 83.3 %copy-start.20 = (bf16[320,1536]{1,0:T(8,128)(2,1)}, bf16[320,1536]{1,0:T(8,128)(2,1)S(1)}, u32[]{:S(2)}) copy-start(bf16[320,1536]{1,0:T(8,128)(2,1)S(1)} %collective-permute-done.7.refs_9_.refs_6_) | copy-start | bytes 2949124
  156.4 59.4 %collective-permute-start.25 = (bf16[320,1536]{1,0:T(8,128)(2,1)S(1)}, bf16[320,1536]{1,0:T(8,128)(2,1)}, u32[]{:S(2)}, u32[]{:S(2)}) collective-permute-start(bf16[320,1536]{1,0:T(8,128)(2,1)S(1)} %collective-permute-done.21.refs_3_.refs_4_), channel_id=1, source_target_pairs={{0,8},{4,12},{8,0},{12,4},{1,9},{5,13},{9,1},{13,5},{2,10},{6,14},... | collective-permute-start | bytes 2949128 | tf_op jit(solution)/shard_map/ppermute | solution.py:278
  156.9 82.8 %copy-start.22 = (bf16[320,1536]{1,0:T(8,128)(2,1)}, bf16[320,1536]{1,0:T(8,128)(2,1)S(1)}, u32[]{:S(2)}) copy-start(bf16[320,1536]{1,0:T(8,128)(2,1)S(1)} %collective-permute-done.8.refs_10_.refs_7_) | copy-start | bytes 2949124
  156.9 79.5 %collective-permute-start.26 = (bf16[320,1536]{1,0:T(8,128)(2,1)S(1)}, bf16[320,1536]{1,0:T(8,128)(2,1)}, u32[]{:S(2)}, u32[]{:S(2)}) collective-permute-start(bf16[320,1536]{1,0:T(8,128)(2,1)S(1)} %collective-permute-done.22.refs_4_.refs_5_), channel_id=1, source_target_pairs={{0,8},{4,12},{8,0},{12,4},{1,9},{5,13},{9,1},{13,5},{2,10},{6,14},... | collective-permute-start | bytes 2949128 | tf_op jit(solution)/shard_map/ppermute | solution.py:278
  173.7 62.7 %collective-permute-start.28 = (bf16[320,1536]{1,0:T(8,128)(2,1)S(1)}, bf16[320,1536]{1,0:T(8,128)(2,1)S(1)}, u32[]{:S(2)}, u32[]{:S(2)}) collective-permute-start(bf16[320,1536]{1,0:T(8,128)(2,1)S(1)} %collective-permute-done.20.refs_2_.refs_3_), channel_id=1, source_target_pairs={{0,4},{4,0},{8,12},{12,8},{1,5},{5,1},{9,13},{13,9},{2,6},{6,2},{1... | collective-permute-start | bytes 2949128 | tf_op jit(solution)/shard_map/ppermute | solution.py:278
  173.7 66.0 %copy-start.24 = (bf16[320,1536]{1,0:T(8,128)(2,1)}, bf16[320,1536]{1,0:T(8,128)(2,1)S(1)}, u32[]{:S(2)}) copy-start(bf16[320,1536]{1,0:T(8,128)(2,1)S(1)} %collective-permute-done.11.refs_13_.refs_10_) | copy-start | bytes 2949124
  173.7 63.2 %collective-permute-start.29 = (bf16[320,1536]{1,0:T(8,128)(2,1)S(1)}, bf16[320,1536]{1,0:T(8,128)(2,1)S(1)}, u32[]{:S(2)}, u32[]{:S(2)}) collective-permute-start(bf16[320,1536]{1,0:T(8,128)(2,1)S(1)} %collective-permute-done.21.refs_3_.refs_4_), channel_id=1, source_target_pairs={{0,4},{4,0},{8,12},{12,8},{1,5},{5,1},{9,13},{13,9},{2,6},{6,2},{1... | collective-permute-start | bytes 2949128 | tf_op jit(solution)/shard_map/ppermute | solution.py:278
  194.7 52.8 %copy-start.6 = (bf16[320,1536]{1,0:T(8,128)(2,1)}, bf16[320,1536]{1,0:T(8,128)(2,1)S(1)}, u32[]{:S(2)}) copy-start(bf16[320,1536]{1,0:T(8,128)(2,1)S(1)} %collective-permute-done.24.refs_6_.refs_7_) | copy-start | bytes 2949124
  194.7 42.4 %collective-permute-start.30 = (bf16[320,1536]{1,0:T(8,128)(2,1)S(1)}, bf16[320,1536]{1,0:T(8,128)(2,1)S(1)}, u32[]{:S(2)}, u32[]{:S(2)}) collective-permute-start(bf16[320,1536]{1,0:T(8,128)(2,1)S(1)} %collective-permute-done.22.refs_4_.refs_5_), channel_id=1, source_target_pairs={{0,4},{4,0},{8,12},{12,8},{1,5},{5,1},{9,13},{13,9},{2,6},{6,2},{1... | collective-permute-start | bytes 2949128 | tf_op jit(solution)/shard_map/ppermute | solution.py:278
  215.9 44.1 %collective-permute-start = (bf16[256,5120]{1,0:T(8,128)(2,1)}, bf16[256,5120]{1,0:T(8,128)(2,1)}, u32[]{:S(2)}, u32[]{:S(2)}) collective-permute-start(bf16[256,5120]{1,0:T(8,128)(2,1)} %fusion.2.refs_0_), channel_id=1, source_target_pairs={{1,2},{2,1},{5,6},{6,5},{9,10},{10,9},{13,14},{14,13},{17,18},{18,... | collective-permute-start | bytes 7864328 | tf_op jit(solution)/shard_map/ppermute | solution.py:275
  236.5 3.2 collective-permute-start.31
  236.5 7.2 %collective-permute-start.32 = (bf16[320,1536]{1,0:T(8,128)(2,1)S(1)}, bf16[320,1536]{1,0:T(8,128)(2,1)}, u32[]{:S(2)}, u32[]{:S(2)}) collective-permute-start(bf16[320,1536]{1,0:T(8,128)(2,1)S(1)} %collective-permute-done.24.refs_6_.refs_7_), channel_id=1, source_target_pairs={{0,4},{4,0},{8,12},{12,8},{1,5},{5,1},{9,13},{13,9},{2,6},{6,2},{1... | collective-permute-start | bytes 2949128 | tf_op jit(solution)/shard_map/ppermute | solution.py:278
  237.0 6.9 %collective-permute-start.33 = (bf16[320,1536]{1,0:T(8,128)(2,1)}, bf16[320,1536]{1,0:T(8,128)(2,1)}, u32[]{:S(2)}, u32[]{:S(2)}) collective-permute-start(bf16[320,1536]{1,0:T(8,128)(2,1)} %collective-permute-done.25.refs_7_.refs_8_), channel_id=1, source_target_pairs={{0,4},{4,0},{8,12},{12,8},{1,5},{5,1},{9,13},{13,9},{2,6},{6,2},{1... | collective-permute-start | bytes 2949128 | tf_op jit(solution)/shard_map/ppermute | solution.py:278
  237.1 7.2 %collective-permute-start.34 = (bf16[320,1536]{1,0:T(8,128)(2,1)}, bf16[320,1536]{1,0:T(8,128)(2,1)}, u32[]{:S(2)}, u32[]{:S(2)}) collective-permute-start(bf16[320,1536]{1,0:T(8,128)(2,1)} %collective-permute-done.26.refs_8_.refs_9_), channel_id=1, source_target_pairs={{0,4},{4,0},{8,12},{12,8},{1,5},{5,1},{9,13},{13,9},{2,6},{6,2},{1... | collective-permute-start | bytes 2949128 | tf_op jit(solution)/shard_map/ppermute | solution.py:278
  240.7 19.4 %collective-permute-start.18 = (bf16[128,5120]{1,0:T(8,128)(2,1)}, bf16[128,5120]{1,0:T(8,128)(2,1)}, u32[]{:S(2)}, u32[]{:S(2)}) collective-permute-start(bf16[128,5120]{1,0:T(8,128)(2,1)} %collective-permute-done.1.refs_2_.refs_0_), channel_id=1, source_target_pairs={{1,2},{2,1},{5,6},{6,5},{9,10},{10,9},{13,14},{14,13},{17,18},{18,... | collective-permute-start | bytes 3932168 | tf_op jit(solution)/shard_map/ppermute | solution.py:275
  243.7 15.6 %collective-permute-start.12 = (bf16[320,1536]{1,0:T(8,128)(2,1)}, bf16[320,1536]{1,0:T(8,128)(2,1)S(1)}, u32[]{:S(2)}, u32[]{:S(2)}) collective-permute-start(bf16[320,1536]{1,0:T(8,128)(2,1)} %copy-done.14), channel_id=1, source_target_pairs={{0,4},{4,0},{8,12},{12,8},{1,5},{5,1},{9,13},{13,9},{2,6},{6,2},{1... | collective-permute-start | bytes 2949128 | tf_op jit(solution)/shard_map/ppermute | solution.py:278
  243.9 15.7 %collective-permute-start.13 = (bf16[320,1536]{1,0:T(8,128)(2,1)}, bf16[320,1536]{1,0:T(8,128)(2,1)S(1)}, u32[]{:S(2)}, u32[]{:S(2)}) collective-permute-start(bf16[320,1536]{1,0:T(8,128)(2,1)} %copy-done.15), channel_id=1, source_target_pairs={{0,4},{4,0},{8,12},{12,8},{1,5},{5,1},{9,13},{13,9},{2,6},{6,2},{1... | collective-permute-start | bytes 2949128 | tf_op jit(solution)/shard_map/ppermute | solution.py:278
  244.3 40.2 %collective-permute-start.19 = (bf16[128,5120]{1,0:T(8,128)(2,1)}, bf16[128,5120]{1,0:T(8,128)(2,1)S(1)}, u32[]{:S(2)}, u32[]{:S(2)}) collective-permute-start(bf16[128,5120]{1,0:T(8,128)(2,1)} %collective-permute-done.2.refs_3_.refs_1_), channel_id=1, source_target_pairs={{1,2},{2,1},{5,6},{6,5},{9,10},{10,9},{13,14},{14,13},{17,18},{18,... | collective-permute-start | bytes 3932168 | tf_op jit(solution)/shard_map/ppermute | solution.py:275
  247.5 12.0 %copy-start.21 = (bf16[320,1536]{1,0:T(8,128)(2,1)S(1)}, bf16[320,1536]{1,0:T(8,128)(2,1)}, u32[]{:S(2)}) copy-start(bf16[320,1536]{1,0:T(8,128)(2,1)} %copy-done.20) | copy-start | bytes 2949124
  247.5 12.5 %copy-start.23 = (bf16[320,1536]{1,0:T(8,128)(2,1)S(1)}, bf16[320,1536]{1,0:T(8,128)(2,1)}, u32[]{:S(2)}) copy-start(bf16[320,1536]{1,0:T(8,128)(2,1)} %copy-done.22) | copy-start | bytes 2949124
  259.3 47.4 %collective-permute-start.14 = (bf16[320,1536]{1,0:T(8,128)(2,1)S(1)}, bf16[320,1536]{1,0:T(8,128)(2,1)S(1)}, u32[]{:S(2)}, u32[]{:S(2)}) collective-permute-start(bf16[320,1536]{1,0:T(8,128)(2,1)S(1)} %copy-done.18), channel_id=1, source_target_pairs={{0,4},{4,0},{8,12},{12,8},{1,5},{5,1},{9,13},{13,9},{2,6},{6,2},{1... | collective-permute-start | bytes 2949128 | tf_op jit(solution)/shard_map/ppermute | solution.py:278
  259.5 48.5 %collective-permute-start.15 = (bf16[320,1536]{1,0:T(8,128)(2,1)S(1)}, bf16[320,1536]{1,0:T(8,128)(2,1)S(1)}, u32[]{:S(2)}, u32[]{:S(2)}) collective-permute-start(bf16[320,1536]{1,0:T(8,128)(2,1)S(1)} %copy-done.21), channel_id=1, source_target_pairs={{0,4},{4,0},{8,12},{12,8},{1,5},{5,1},{9,13},{13,9},{2,6},{6,2},{1... | collective-permute-start | bytes 2949128 | tf_op jit(solution)/shard_map/ppermute | solution.py:278
  260.0 49.4 %collective-permute-start.16 = (bf16[320,1536]{1,0:T(8,128)(2,1)S(1)}, bf16[320,1536]{1,0:T(8,128)(2,1)S(1)}, u32[]{:S(2)}, u32[]{:S(2)}) collective-permute-start(bf16[320,1536]{1,0:T(8,128)(2,1)S(1)} %copy-done.23), channel_id=1, source_target_pairs={{0,4},{4,0},{8,12},{12,8},{1,5},{5,1},{9,13},{13,9},{2,6},{6,2},{1... | collective-permute-start | bytes 2949128 | tf_op jit(solution)/shard_map/ppermute | solution.py:278
  260.3 50.4 %collective-permute-start.17 = (bf16[320,1536]{1,0:T(8,128)(2,1)}, bf16[320,1536]{1,0:T(8,128)(2,1)}, u32[]{:S(2)}, u32[]{:S(2)}) collective-permute-start(bf16[320,1536]{1,0:T(8,128)(2,1)} %collective-permute-done.9.refs_11_.refs_8_), channel_id=1, source_target_pairs={{0,4},{4,0},{8,12},{12,8},{1,5},{5,1},{9,13},{13,9},{2,6},{6,2},{1... | collective-permute-start | bytes 2949128 | tf_op jit(solution)/shard_map/ppermute | solution.py:278
  284.5 54.7 %collective-permute-start.37 = (bf16[128,1536]{1,0:T(8,128)(2,1)S(1)}, bf16[128,1536]{1,0:T(8,128)(2,1)S(1)}, u32[]{:S(2)}, u32[]{:S(2)}) collective-permute-start(bf16[128,1536]{1,0:T(8,128)(2,1)S(1)} %get-tuple-element.15), channel_id=1, source_target_pairs={{1,0},{2,3},{5,4},{6,7},{9,8},{10,11},{13,12},{14,15},{17,16},{18,... | collective-permute-start | bytes 1179656 | tf_op jit(solution)/shard_map/ppermute | solution.py:275
  306.8 33.7 %copy-start.27 = (bf16[320,1536]{1,0:T(8,128)(2,1)}, bf16[320,1536]{1,0:T(8,128)(2,1)S(1)}, u32[]{:S(2)}) copy-start(bf16[320,1536]{1,0:T(8,128)(2,1)S(1)} %collective-permute-done.14.refs_16_.refs_13_) | copy-start | bytes 2949124
  306.8 105.2 %collective-permute-start.35 = (bf16[256,1536]{1,0:T(8,128)(2,1)S(1)}, bf16[256,1536]{1,0:T(8,128)(2,1)S(1)}, u32[]{:S(2)}, u32[]{:S(2)}) collective-permute-start(bf16[256,1536]{1,0:T(8,128)(2,1)S(1)} %project.11), channel_id=1, source_target_pairs={{1,0},{2,3},{5,4},{6,7},{9,8},{10,11},{13,12},{14,15},{17,16},{18,... | collective-permute-start | bytes 2359304 | tf_op jit(solution)/shard_map/ppermute | solution.py:275
  308.1 32.4 %copy-start.28 = (bf16[320,1536]{1,0:T(8,128)(2,1)}, bf16[320,1536]{1,0:T(8,128)(2,1)S(1)}, u32[]{:S(2)}) copy-start(bf16[320,1536]{1,0:T(8,128)(2,1)S(1)} %collective-permute-done.15.refs_17_.refs_14_) | copy-start | bytes 2949124
  308.1 103.9 %collective-permute-start.36 = (bf16[256,1536]{1,0:T(8,128)(2,1)S(1)}, bf16[256,1536]{1,0:T(8,128)(2,1)S(1)}, u32[]{:S(2)}, u32[]{:S(2)}) collective-permute-start(bf16[256,1536]{1,0:T(8,128)(2,1)S(1)} %project.12), channel_id=1, source_target_pairs={{1,0},{2,3},{5,4},{6,7},{9,8},{10,11},{13,12},{14,15},{17,16},{18,... | collective-permute-start | bytes 2359304 | tf_op jit(solution)/shard_map/ppermute | solution.py:275
  309.4 31.1 %copy-start.29 = (bf16[320,1536]{1,0:T(8,128)(2,1)}, bf16[320,1536]{1,0:T(8,128)(2,1)S(1)}, u32[]{:S(2)}) copy-start(bf16[320,1536]{1,0:T(8,128)(2,1)S(1)} %collective-permute-done.16.refs_18_.refs_15_) | copy-start | bytes 2949124
  309.4 88.3 %collective-permute-start.38 = (bf16[128,1536]{1,0:T(8,128)(2,1)S(1)}, bf16[128,1536]{1,0:T(8,128)(2,1)S(1)}, u32[]{:S(2)}, u32[]{:S(2)}) collective-permute-start(bf16[128,1536]{1,0:T(8,128)(2,1)S(1)} %get-tuple-element.16), channel_id=1, source_target_pairs={{1,0},{2,3},{5,4},{6,7},{9,8},{10,11},{13,12},{14,15},{17,16},{18,... | collective-permute-start | bytes 1179656 | tf_op jit(solution)/shard_map/ppermute | solution.py:275
  310.7 95.4 %collective-permute-start.39 = (bf16[128,1536]{1,0:T(8,128)(2,1)S(1)}, bf16[128,1536]{1,0:T(8,128)(2,1)S(1)}, u32[]{:S(2)}, u32[]{:S(2)}) collective-permute-start(bf16[128,1536]{1,0:T(8,128)(2,1)S(1)} %project.14), channel_id=1, source_target_pairs={{1,0},{2,3},{5,4},{6,7},{9,8},{10,11},{13,12},{14,15},{17,16},{18,... | collective-permute-start | bytes 1179656 | tf_op jit(solution)/shard_map/ppermute | solution.py:275
  339.2 72.8 %collective-permute-start.40 = (bf16[128,1536]{1,0:T(8,128)(2,1)S(1)}, bf16[128,1536]{1,0:T(8,128)(2,1)S(1)}, u32[]{:S(2)}, u32[]{:S(2)}) collective-permute-start(bf16[128,1536]{1,0:T(8,128)(2,1)S(1)} %project.15), channel_id=1, source_target_pairs={{1,0},{2,3},{5,4},{6,7},{9,8},{10,11},{13,12},{14,15},{17,16},{18,... | collective-permute-start | bytes 1179656 | tf_op jit(solution)/shard_map/ppermute | solution.py:275
  397.7 14.3 %copy-start.35 = (bf16[128,1536]{1,0:T(8,128)(2,1)}, bf16[128,1536]{1,0:T(8,128)(2,1)S(1)}, u32[]{:S(2)}) copy-start(bf16[128,1536]{1,0:T(8,128)(2,1)S(1)} %collective-permute-done.38.refs_9_) | copy-start | bytes 1179652
  (15 other events, 66.8 us)

commit v4 on v3

--- a/solution.py
+++ b/solution.py
@@ -71,84 +71,94 @@
     return attend(qkv, q_gain, k_gain, lengths[0])
 
 
-def project_kernel(blocks, tile, scal, *refs):
+def project_kernel(blocks, bases, tile, scal, *refs):
     rows_refs = refs[:blocks]
     pieces = refs[blocks : blocks + 16]
     cos_ref, sin_ref, gain_ref = refs[blocks + 16 : blocks + 19]
     outs = refs[blocks + 19 : 2 * blocks + 19]
-    held, total, sems = refs[2 * blocks + 19 :]
-    depth, columns = pieces[0].shape
-    band = 4 * depth
-
-    def copy(index):
-        group, slot = divmod(index, 4)
-        start = pl.multiple_of(scal[slot] * depth, 16)
-        return pltpu.make_async_copy(
-            pieces[index], held.at[group, pl.ds(start, depth), :], sems.at[index]
+    taken, held, row_sems, sems = refs[2 * blocks + 19 :]
+    depth = pieces[0].shape[0]
+    columns = outs[0].shape[1]
+    steps = columns // tile
+
+    def copies(step):
+        made = []
+        for index in range(16):
+            start = pl.multiple_of((scal[4 + index // 4] * 4 + scal[index % 4]) * depth, 16)
+            low = bases[index] + step * tile
+            made.append(
+                pltpu.make_async_copy(
+                    pieces[index].at[:, low : low + tile],
+                    held.at[step % 2, pl.ds(start, depth), :],
+                    sems.at[step % 2, index],
+                )
+            )
+        return made
+
+    row_copies = []
+    first = 0
+    for number, ref in enumerate(rows_refs):
+        rows = ref.shape[0]
+        row_copies.append(
+            pltpu.make_async_copy(ref, taken.at[first : first + rows, :], row_sems.at[number])
         )
-
-    for index in range(16):
-        copy(index).start()
-    for group in range(4):
-        for slot in range(4):
-            copy(4 * group + slot).wait()
-        offset = pl.multiple_of(scal[4 + group] * band, 128)
+        first += rows
+    for copy in copies(0) + row_copies:
+        copy.start()
+    for step in range(steps):
+        if step + 1 < steps:
+            for copy in copies(step + 1):
+                copy.start()
+        if step == 0:
+            for copy in row_copies:
+                copy.wait()
+        for copy in copies(step):
+            copy.wait()
+        total = jnp.dot(taken[...], held[step % 2], preferred_element_type=jnp.float32)
         first = 0
-        for ref in rows_refs:
-            rows = ref.shape[0]
-
-            @pl.loop(0, columns // tile)
-            def _(step, ref=ref, first=first, rows=rows):
-                at = pl.ds(pl.multiple_of(step * tile, tile), tile)
-                part = jnp.dot(
-                    ref[:, pl.ds(offset, band)],
-                    held[group, :, at],
-                    preferred_element_type=jnp.float32,
-                )
-                if group:
-                    part = part + total[first : first + rows, at]
-                total[first : first + rows, at] = part
-
+        for number, out in enumerate(outs):
+            rows = out.shape[0]
+            place = pl.ds(pl.multiple_of(scal[8 + number], 128), rows)
+            cosine = cos_ref[place, :]
+            sine = sin_ref[place, :]
+            for head in range(tile // HD):
+                kind = (step * (tile // HD) + head) % (GQ + 2)
+                vec = total[first : first + rows, head * HD : (head + 1) * HD]
+                if kind <= GQ:
+                    scale = lax.rsqrt(jnp.mean(vec * vec, axis=-1, keepdims=True) + 1e-06)
+                    gain = gain_ref[0:1, :] if kind < GQ else gain_ref[1:2, :]
+                    vec = vec * scale * gain
+                    vec = vec * cosine + pltpu.roll(vec, HD // 2, 1) * sine
+                at = step * tile + head * HD
+                out[:, at : at + HD] = vec.astype(out.dtype)
             first += rows
-    first = 0
-    for number, (ref, out) in enumerate(zip(rows_refs, outs)):
-        rows = ref.shape[0]
-        place = pl.ds(pl.multiple_of(scal[8 + number], 128), rows)
-        cosine = cos_ref[place, :]
-        sine = sin_ref[place, :]
-        for head in range(columns // HD):
-            kind = head % (GQ + 2)
-            at = slice(head * HD, (head + 1) * HD)
-            vec = total[first : first + rows, at]
-            if kind <= GQ:
-                scale = lax.rsqrt(jnp.mean(vec * vec, axis=-1, keepdims=True) + 1e-06)
-                gain = gain_ref[0:1, :] if kind < GQ else gain_ref[1:2, :]
-                vec = vec * scale * gain
-                vec = vec * cosine + pltpu.roll(vec, HD // 2, 1) * sine
-            out[:, at] = vec.astype(out.dtype)
-        first += rows
 
 
 def project(rows_list, places, pieces, scal, cos, sin, gains):
     blocks = len(rows_list)
-    columns = pieces[0].shape[1]
-    depth = pieces[0].shape[0]
+    arrays = [p for p, _ in pieces]
+    bases = [base for _, base in pieces]
+    columns = min(p.shape[1] for p in arrays)
+    depth = arrays[0].shape[0]
+    tile = columns // 3
     count = sum(r.shape[0] for r in rows_list)
     width = rows_list[0].shape[1]
     scal = jnp.concatenate([scal, jnp.stack(places)]).astype(jnp.int32)
     vmem = pl.BlockSpec(memory_space=pltpu.VMEM)
+    hbm = pl.BlockSpec(memory_space=pl.ANY)
     return pl.pallas_call(
-        functools.partial(project_kernel, blocks, 512),
+        functools.partial(project_kernel, blocks, bases, tile),
         out_shape=[jax.ShapeDtypeStruct((r.shape[0], columns), jnp.bfloat16) for r in rows_list],
         in_specs=[pl.BlockSpec(memory_space=pltpu.SMEM)]
-        + [vmem] * blocks
-        + [pl.BlockSpec(memory_space=pl.ANY)] * 16
+        + [hbm] * blocks
+        + [hbm] * 16
         + [vmem] * 3,
         out_specs=[vmem] * blocks,
         scratch_shapes=[
-            pltpu.VMEM((4, 4 * depth, columns), jnp.bfloat16),
-            pltpu.VMEM((count, columns), jnp.float32),
-            pltpu.SemaphoreType.DMA((16,)),
+            pltpu.VMEM((count, width), jnp.bfloat16),
+            pltpu.VMEM((2, width, tile), jnp.bfloat16),
+            pltpu.SemaphoreType.DMA((blocks,)),
+            pltpu.SemaphoreType.DMA((2, 16)),
         ],
         compiler_params=pltpu.CompilerParams(vmem_limit_bytes=VMEM_BYTES),
         cost_estimate=pl.CostEstimate(
@@ -157,7 +167,7 @@
             transcendentals=0,
         ),
         name="project",
-    )(scal, *rows_list, *pieces, cos, sin, gains)
+    )(scal, *rows_list, *arrays, cos, sin, gains)
 
 
 def attend_kernel(parts, block, scal, *refs):
@@ -257,6 +267,10 @@
     )(scal, *near, *far)
 
 
+def after(x, *earlier):
+    return lax.optimization_barrier((x,) + earlier)[0]
+
+
 def four_planes(tokens, w_qkv, norm_gain, q_gain, k_gain, lengths):
     t = lax.axis_index("tensor")
     f = lax.axis_index("fsdp")
@@ -282,20 +296,53 @@
     far = [(0, 2), (3, 1)]
     outward = [(1, 0), (2, 3)]
 
-    def collect(same, other):
-        mine = [same, across(same, inward), across(other, swap), across(other, far)]
-        over = [beside(x, 2) for x in mine]
-        return mine + over + [beside(x, 1) for x in mine] + [beside(x, 1) for x in over]
-
-    end_pieces = collect(slab(end), slab(far_end))
-    mid_pieces = collect(slab(mid), slab(far_mid))
-    scal = jnp.stack([mid, end, far_mid, far_end] + [jnp.bitwise_xor(f, m) for m in (0, 2, 1, 3)])
-
+    same = jnp.concatenate([slab(end), slab(mid)], axis=1)
+    other = jnp.concatenate([slab(far_end), slab(far_mid)], axis=1)
     normed = head_norm(tokens.astype(jnp.float32), norm_gain).astype(jnp.bfloat16)
     half = rows // 2
-    near_rows = [across(normed[:half], inward), across(normed[half:], inward)]
-    swap_rows = across(normed, swap)
-    far_rows = [across(x, swap) for x in near_rows]
+
+    from_swap = across(other, swap)
+    from_end = across(same, inward)
+    over_mine = beside(same, 2)
+    core_mine = beside(same, 1)
+    from_far_e = across(after(other[:, :columns], from_swap), far)
+    rows_a1 = across(after(normed[:half], from_end), inward)
+    over_swap_e = beside(after(from_swap[:, :columns], over_mine), 2)
+    over_end_e = beside(after(from_end[:, :columns], over_mine), 2)
+    core_swap = beside(from_swap, 1)
+    core_end = beside(from_end, 1)
+    core_over = beside(over_mine, 1)
+    from_far_o = across(after(other[:, columns:], from_far_e), far)
+    rows_b = across(after(normed, from_far_e), swap)
+    rows_a2 = across(after(normed[half:], rows_a1), inward)
+    over_far_e = beside(after(from_far_e, over_swap_e, over_end_e), 2)
+    core_far_e = beside(from_far_e, 1)
+    core_over_swap_e = beside(over_swap_e, 1)
+    core_over_end_e = beside(over_end_e, 1)
+    rows_c1 = across(after(rows_a1, from_far_o), swap)
+    over_swap_o = beside(after(from_swap[:, columns:], over_far_e), 2)
+    over_end_o = beside(after(from_end[:, columns:], over_far_e), 2)
+    core_over_far_e = beside(over_far_e, 1)
+    core_far_o = beside(from_far_o, 1)
+    rows_c2 = across(after(rows_a2, rows_b), swap)
+    over_far_o = beside(after(from_far_o, over_swap_o), 2)
+    core_over_swap_o = beside(over_swap_o, 1)
+    core_over_end_o = beside(over_end_o, 1)
+    core_over_far_o = beside(over_far_o, 1)
+
+    end_pieces = [
+        (same, 0), (from_end, 0), (from_swap, 0), (from_far_e, 0),
+        (over_mine, 0), (over_end_e, 0), (over_swap_e, 0), (over_far_e, 0),
+        (core_mine, 0), (core_end, 0), (core_swap, 0), (core_far_e, 0),
+        (core_over, 0), (core_over_end_e, 0), (core_over_swap_e, 0), (core_over_far_e, 0),
+    ]
+    mid_pieces = [
+        (same, columns), (from_end, columns), (from_swap, columns), (from_far_o, 0),
+        (over_mine, columns), (over_end_o, 0), (over_swap_o, 0), (over_far_o, 0),
+        (core_mine, columns), (core_end, columns), (core_swap, columns), (core_far_o, 0),
+        (core_over, columns), (core_over_end_o, 0), (core_over_swap_o, 0), (core_over_far_o, 0),
+    ]
+    scal = jnp.stack([mid, end, far_mid, far_end] + [jnp.bitwise_xor(f, m) for m in (0, 2, 1, 3)])
 
     positions = jnp.arange(4 * rows, dtype=jnp.int32)
     angle = angles(positions)
@@ -303,7 +350,7 @@
     sin = jnp.concatenate([-jnp.sin(angle), jnp.sin(angle)], axis=1)
     gains = jnp.stack([q_gain, k_gain])
 
-    blocks = [normed, swap_rows, near_rows[0], near_rows[1], far_rows[0], far_rows[1]]
+    blocks = [normed, rows_b, rows_a1, rows_a2, rows_c1, rows_c2]
     places = [
         mid * rows,
         far_mid * rows,
@@ -319,10 +366,10 @@
         )
 
     sent = []
-    for picked in ([0], [1], [2, 3], [4], [5]):
+    for picked in ([0], [1, 2, 3], [4], [5]):
         sent += [across(x, outward) for x in run(picked, end_pieces)]
     near = []
-    for picked in ([0, 1, 2, 3], [4], [5]):
+    for picked in ([0, 1, 2, 3], [4, 5]):
         near += run(picked, mid_pieces)
     middle = jnp.where((t == 1) | (t == 2), 1, 0)
     return attend_blocks(near, sent, places, middle, lengths[0])

time: 434 us -> 375 us (0.86)
  the two profiles are of different devices: /device:TPU:24 before, /device:TPU:0 now
where the time goes in v4:
time: 375 us; the launch traced here: 371 us
  waiting for transfers between devices  169 us (45%)
  Pallas kernels  105 us (28%)
  starting transfers between devices  83.5 us (22%)
  local copies, waits for them, and re-layouts  6.32 us (2%)
  other arithmetic  4.14 us (1%)
    ppermute x15, waiting for transfers between devices, across(): return lax.ppermute(x, 'tensor', pairs)  100 us
    pallas_call x6, Pallas kernels, project(): pl.pallas_call(functools.partial(project_kernel, blocks, bases, tile), ou...  87.9 us
    ppermute x15, starting transfers between devices, across(): return lax.ppermute(x, 'tensor', pairs)  73.5 us
    ppermute x19, waiting for transfers between devices, beside(): return lax.ppermute(x, 'fsdp', [(i, i ^ bit) for i in range(4)])  69.5 us
    pallas_call x1, Pallas kernels, attend_blocks(): pl.pallas_call(functools.partial(attend_kernel, parts, 256), out_shape=ja...  17.5 us
    ppermute x19, starting transfers between devices, beside(): return lax.ppermute(x, 'fsdp', [(i, i ^ bit) for i in range(4)])  10.1 us
  transfers between devices with their start and end apart: 34, of which 13 were waited for; matrix products, arithmetic and copies ran while one was open for 2% of the time, Pallas kernels for 24%

profile of v4, /device:TPU:0, one launch (start us, length us, event | category | flops | bytes accessed | tf_op | source)
XLA Modules:
  0.0 370.7 jit_solution(8695695168822570831)
XLA Ops:
  0.0 2.4 constant_dynamic-slice_fusion.1
  2.4 0.3 pad_maximum_fusion
  2.6 0.8 collective-permute-start
  3.4 0.3 pad_maximum_fusion.1.refs_4_.refs_2_.refs_1_.refs_3_
  3.7 8.0 %collective-permute-start.3 = (bf16[320,3072]{1,0:T(8,128)(2,1)S(1)}, bf16[320,3072]{1,0:T(8,128)(2,1)S(1)}, u32[]{:S(2)}, u32[]{:S(2)}) collective-permute-start(bf16[320,3072]{1,0:T(8,128)(2,1)S(1)} %pad_maximum_fusion.1.refs_4_.refs_2_.refs_1_.refs_3_), channel_id=1, source_target_pairs={{0,1},{3,2},{4,5},{7,6},{8,9},{11,10},{12,13},{15,14},{16,17},{19,... | collective-permute-start | bytes 5898248 | tf_op jit(solution)/shard_map/ppermute | solution.py:289
  11.7 1.6 collective-permute-start.7
  13.3 0.6 fusion
  13.9 0.8 fusion.2.refs_0_
  14.8 40.3 %collective-permute-start.1 = (bf16[320,1536]{1,0:T(8,128)(2,1)S(1)}, bf16[320,1536]{1,0:T(8,128)(2,1)S(1)}, u32[]{:S(2)}, u32[]{:S(2)}) collective-permute-start(bf16[320,1536]{1,0:T(8,128)(2,1)S(1)} %get-tuple-element.27), channel_id=1, source_target_pairs={{0,2},{3,1},{4,6},{7,5},{8,10},{11,9},{12,14},{15,13},{16,18},{19,... | collective-permute-start | bytes 2949128 | tf_op jit(solution)/shard_map/ppermute | solution.py:289
  55.1 1.3 fusion.6
  56.4 1.5 collective-permute-start.9
  57.9 0.1 fusion.5
  58.0 0.6 collective-permute-start.8
  58.6 0.2 fusion.4
  58.8 3.7 %collective-permute-start.4 = (bf16[128,5120]{1,0:T(8,128)(2,1)S(1)}, bf16[128,5120]{1,0:T(8,128)(2,1)}, u32[]{:S(2)}, u32[]{:S(2)}) collective-permute-start(bf16[128,5120]{1,0:T(8,128)(2,1)S(1)} %get-tuple-element.29), channel_id=1, source_target_pairs={{0,1},{3,2},{4,5},{7,6},{8,9},{11,10},{12,13},{15,14},{16,17},{19,... | collective-permute-start | bytes 3932168 | tf_op jit(solution)/shard_map/ppermute | solution.py:289
  62.5 14.7 %collective-permute-done.1.refs_4_.refs_6_ = bf16[320,1536]{1,0:T(8,128)(2,1)S(1)} collective-permute-done((bf16[320,1536]{1,0:T(8,128)(2,1)S(1)}, bf16[320,1536]{1,0:T(8,128)(2,1)S(1)}, u32[]{:S(2)}, u32[]{:S(2)}) %collective-permute-start.1) | collective-permute-done | bytes 983072 | tf_op jit(solution)/shard_map/ppermute | solution.py:289
  77.2 3.8 %collective-permute-done.9.refs_6_.refs_8_ = bf16[320,1536]{1,0:T(8,128)(2,1)S(1)} collective-permute-done((bf16[320,1536]{1,0:T(8,128)(2,1)S(1)}, bf16[320,1536]{1,0:T(8,128)(2,1)S(1)}, u32[]{:S(2)}, u32[]{:S(2)}) %collective-permute-start.9) | collective-permute-done | bytes 983072 | tf_op jit(solution)/shard_map/ppermute | solution.py:292
  81.1 18.7 %collective-permute-done.8.refs_7_.refs_9_ = bf16[320,1536]{1,0:T(8,128)(2,1)S(1)} collective-permute-done((bf16[320,1536]{1,0:T(8,128)(2,1)S(1)}, bf16[320,1536]{1,0:T(8,128)(2,1)S(1)}, u32[]{:S(2)}, u32[]{:S(2)}) %collective-permute-start.8) | collective-permute-done | bytes 983072 | tf_op jit(solution)/shard_map/ppermute | solution.py:292
  99.8 1.5 collective-permute-start.10
  101.3 0.5 collective-permute-start.18
  101.8 0.1 collective-permute-start.25
  101.9 1.3 collective-permute-done.4.refs_2_.refs_1_
  103.2 18.1 %collective-permute-done.10.refs_8_.refs_10_ = bf16[320,1536]{1,0:T(8,128)(2,1)} collective-permute-done((bf16[320,1536]{1,0:T(8,128)(2,1)S(1)}, bf16[320,1536]{1,0:T(8,128)(2,1)}, u32[]{:S(2)}, u32[]{:S(2)}) %collective-permute-start.10) | collective-permute-done | bytes 983072 | tf_op jit(solution)/shard_map/ppermute | solution.py:292
  121.3 0.8 collective-permute-start.2
  122.1 5.3 %collective-permute-start.6 = (bf16[320,1536]{1,0:T(8,128)(2,1)S(1)}, bf16[320,1536]{1,0:T(8,128)(2,1)S(1)}, u32[]{:S(2)}, u32[]{:S(2)}) collective-permute-start(bf16[320,1536]{1,0:T(8,128)(2,1)S(1)} %get-tuple-element.31), channel_id=1, source_target_pairs={{0,2},{3,1},{4,6},{7,5},{8,10},{11,9},{12,14},{15,13},{16,18},{19,... | collective-permute-start | bytes 2949128 | tf_op jit(solution)/shard_map/ppermute | solution.py:289
  127.6 2.4 collective-permute-start.5
  130.0 1.5 collective-permute-start.12
  131.5 18.1 %collective-permute-done.6.refs_7_.refs_5_ = bf16[320,1536]{1,0:T(8,128)(2,1)S(1)} collective-permute-done((bf16[320,1536]{1,0:T(8,128)(2,1)S(1)}, bf16[320,1536]{1,0:T(8,128)(2,1)S(1)}, u32[]{:S(2)}, u32[]{:S(2)}) %collective-permute-start.6) | collective-permute-done | bytes 983072 | tf_op jit(solution)/shard_map/ppermute | solution.py:289
  149.6 23.7 %collective-permute-done.5.refs_3_.refs_2_ = bf16[128,5120]{1,0:T(8,128)(2,1)} collective-permute-done((bf16[128,5120]{1,0:T(8,128)(2,1)S(1)}, bf16[128,5120]{1,0:T(8,128)(2,1)}, u32[]{:S(2)}, u32[]{:S(2)}) %collective-permute-start.5) | collective-permute-done | bytes 1310752 | tf_op jit(solution)/shard_map/ppermute | solution.py:289
  173.3 2.0 collective-permute-start.22
  175.4 0.9 copy-done.17
  176.3 1.9 collective-permute-start.23
  178.2 0.1 concatenate.45.scal
  178.3 0.1 concatenate.44.scal
  178.4 0.1 concatenate.41.scal
  178.5 0.1 concatenate.42.scal
  178.6 0.1 concatenate.43.scal
  178.7 0.1 concatenate.36.scal
  179.4 0.1 stack.77.scal
  179.6 1.6 collective-permute-start.11
  181.1 0.5 collective-permute-start.13
  181.7 1.9 fusion.3
  183.6 0.3 pad_maximum_fusion.2
  184.0 11.7 %project.8 = bf16[256,1536]{1,0:T(8,128)(2,1)S(1)} custom-call(s32[9]{0:T(128)S(1)} %concatenate.42.scal, bf16[256,5120]{1,0:T(8,128)(2,1)} %copy-done.7, bf16[320,3072]{1,0:T(8,128)(2,1)} %copy-done.1, bf16[320,3072]{1,0:T(8,128)(2,1)} %copy-done.2, bf16[320,3072]{1,0:T(8,128)(2,1)} %copy-done, bf16[320,1536]{1,0:T(8,128)(2,1)} %copy-done.8, ...), custom_call_target="tpu_custom_call" | custom-call | flops 4026531840 | bytes 19136512 | tf_op jit(solution)/shard_map/project/pallas_call | solution.py:149
  195.7 8.6 %collective-permute-done.11.refs_9_.refs_7_ = bf16[320,1536]{1,0:T(8,128)(2,1)S(1)} collective-permute-done((bf16[320,1536]{1,0:T(8,128)(2,1)}, bf16[320,1536]{1,0:T(8,128)(2,1)S(1)}, u32[]{:S(2)}, u32[]{:S(2)}) %collective-permute-start.11) | collective-permute-done | bytes 983072 | tf_op jit(solution)/shard_map/ppermute | solution.py:292
  204.4 0.5 collective-permute-start.19
  204.9 20.2 %collective-permute-done.13.refs_11_.refs_9_ = bf16[320,1536]{1,0:T(8,128)(2,1)S(1)} collective-permute-done((bf16[320,1536]{1,0:T(8,128)(2,1)}, bf16[320,1536]{1,0:T(8,128)(2,1)S(1)}, u32[]{:S(2)}, u32[]{:S(2)}) %collective-permute-start.13) | collective-permute-done | bytes 983072 | tf_op jit(solution)/shard_map/ppermute | solution.py:292
  225.1 9.8 %project.10 = bf16[128,1536]{1,0:T(8,128)(2,1)S(1)} custom-call(s32[9]{0:T(128)S(1)} %concatenate.44.scal, bf16[128,5120]{1,0:T(8,128)(2,1)} %collective-permute-done.22.refs_0_, bf16[320,3072]{1,0:T(8,128)(2,1)} %copy-done.1, bf16[320,3072]{1,0:T(8,128)(2,1)} %copy-done.2, bf16[320,3072]{1,0:T(8,128)(2,1)} %copy-done, bf16[320,1536]{1,0:T(8,128)(2,1)} %copy-done.8, ...), custom_call_target="tpu_custom_call" | custom-call | flops 2013265920 | bytes 17432576 | tf_op jit(solution)/shard_map/project/pallas_call | solution.py:149
  234.9 1.5 collective-permute-start.32
  236.4 18.6 %project.9 = (bf16[256,1536]{1,0:T(8,128)(2,1)}, bf16[128,1536]{1,0:T(8,128)(2,1)S(1)}, bf16[128,1536]{1,0:T(8,128)(2,1)S(1)}) custom-call(s32[11]{0:T(128)S(1)} %concatenate.43.scal, bf16[256,5120]{1,0:T(8,128)(2,1)} %copy-done.14, bf16[128,5120]{1,0:T(8,128)(2,1)} %collective-permute-done.4.refs_2_.refs_1_, ...), custom_call_target="tpu_custom_call" | custom-call | flops 8053063680 | bytes 22544384 | tf_op jit(solution)/shard_map/project/pallas_call | solution.py:149
  255.1 9.8 %project.11 = bf16[128,1536]{1,0:T(8,128)(2,1)S(1)} custom-call(s32[9]{0:T(128)S(1)} %concatenate.45.scal, bf16[128,5120]{1,0:T(8,128)(2,1)} %collective-permute-done.23.refs_1_.refs_0_, bf16[320,3072]{1,0:T(8,128)(2,1)} %copy-done.1, bf16[320,3072]{1,0:T(8,128)(2,1)} %copy-done.2, bf16[320,3072]{1,0:T(8,128)(2,1)} %copy-done, bf16[320,1536]{1,0:T(8,128)(2,1)} %copy-done.8, ...), custom_call_target="tpu_custom_call" | custom-call | flops 2013265920 | bytes 17432576 | tf_op jit(solution)/shard_map/project/pallas_call | solution.py:149
  264.9 1.3 collective-permute-start.28
  266.2 5.1 %collective-permute-done.32.refs_10_ = bf16[128,1536]{1,0:T(8,128)(2,1)S(1)} collective-permute-done((bf16[128,1536]{1,0:T(8,128)(2,1)S(1)}, bf16[128,1536]{1,0:T(8,128)(2,1)S(1)}, u32[]{:S(2)}, u32[]{:S(2)}) %collective-permute-start.32) | collective-permute-done | bytes 393248 | tf_op jit(solution)/shard_map/ppermute | solution.py:289
  271.3 1.3 collective-permute-start.29
  272.7 1.3 collective-permute-start.30
  274.0 1.3 collective-permute-start.31
  275.3 1.5 collective-permute-start.33
  276.9 26.3 %project.6 = (bf16[256,1536]{1,0:T(8,128)(2,1)}, bf16[256,1536]{1,0:T(8,128)(2,1)}, bf16[128,1536]{1,0:T(8,128)(2,1)S(1)}, bf16[128,1536]{1,0:T(8,128)(2,1)S(1)}) custom-call(s32[12]{0:T(128)S(1)} %concatenate.36.scal, bf16[256,5120]{1,0:T(8,128)(2,1)} %copy-done.7, bf16[256,5120]{1,0:T(8,128)(2,1)} %copy-done.14, ...), custom_call_target="tpu_custom_call" | custom-call | flops 12079595520 | bytes 25952256 | tf_op jit(solution)/shard_map/project/pallas_call | solution.py:149
  303.2 11.7 %project.7 = (bf16[128,1536]{1,0:T(8,128)(2,1)S(1)}, bf16[128,1536]{1,0:T(8,128)(2,1)S(1)}) custom-call(s32[10]{0:T(128)S(1)} %concatenate.41.scal, bf16[128,5120]{1,0:T(8,128)(2,1)} %collective-permute-done.22.refs_0_, bf16[128,5120]{1,0:T(8,128)(2,1)} %collective-permute-done.23.refs_1_.refs_0_, bf16[320,3072]{1,0:T(8,128)(2,1)} %copy-done.1, ...), custom_call_target="tpu_custom_call" | custom-call | flops 4026531840 | bytes 19136512 | tf_op jit(solution)/shard_map/project/pallas_call | solution.py:149
  314.9 20.4 %collective-permute-done.30.refs_8_ = bf16[128,1536]{1,0:T(8,128)(2,1)S(1)} collective-permute-done((bf16[128,1536]{1,0:T(8,128)(2,1)S(1)}, bf16[128,1536]{1,0:T(8,128)(2,1)S(1)}, u32[]{:S(2)}, u32[]{:S(2)}) %collective-permute-start.30) | collective-permute-done | bytes 393248 | tf_op jit(solution)/shard_map/ppermute | solution.py:289
  335.3 8.4 %collective-permute-done.31.refs_9_ = bf16[128,1536]{1,0:T(8,128)(2,1)S(1)} collective-permute-done((bf16[128,1536]{1,0:T(8,128)(2,1)S(1)}, bf16[128,1536]{1,0:T(8,128)(2,1)S(1)}, u32[]{:S(2)}, u32[]{:S(2)}) %collective-permute-start.31) | collective-permute-done | bytes 393248 | tf_op jit(solution)/shard_map/ppermute | solution.py:289
  343.7 8.2 %collective-permute-done.33.refs_11_ = bf16[128,1536]{1,0:T(8,128)(2,1)S(1)} collective-permute-done((bf16[128,1536]{1,0:T(8,128)(2,1)S(1)}, bf16[128,1536]{1,0:T(8,128)(2,1)S(1)}, u32[]{:S(2)}, u32[]{:S(2)}) %collective-permute-start.33) | collective-permute-done | bytes 393248 | tf_op jit(solution)/shard_map/ppermute | solution.py:289
  351.9 0.7 copy-done.30
  352.7 17.5 %attend.1 = bf16[1024,1024]{1,0:T(8,128)(2,1)} custom-call(s32[8]{0:T(128)S(1)} %stack.77.scal, bf16[256,1536]{1,0:T(8,128)(2,1)} %get-tuple-element.38.refs_0_, bf16[256,1536]{1,0:T(8,128)(2,1)} %get-tuple-element.39.refs_1_, bf16[128,1536]{1,0:T(8,128)(2,1)S(1)} %get-tuple-element.40.refs_2_, bf16[128,1536]{1,0:T(8,128)(2,1)S(1)} %get-tuple-element.41.refs_3_, ...), custom_call_target="tpu_custom_call" | custom-call | flops 4294967296 | bytes 5242880 | tf_op jit(solution)/shard_map/attend/pallas_call | solution.py:250
  (94 shorter events, 0.4 us)
Async XLA Ops:
  2.6 12.1 %collective-permute-start = (bf16[320,3072]{1,0:T(8,128)(2,1)S(1)}, bf16[320,3072]{1,0:T(8,128)(2,1)S(1)}, u32[]{:S(2)}, u32[]{:S(2)}) collective-permute-start(bf16[320,3072]{1,0:T(8,128)(2,1)S(1)} %pad_maximum_fusion), channel_id=1, source_target_pairs={{1,2},{2,1},{5,6},{6,5},{9,10},{10,9},{13,14},{14,13},{17,18},{18,... | collective-permute-start | bytes 5898248 | tf_op jit(solution)/shard_map/ppermute | solution.py:289
  3.4 9.9 %copy-start.13 = (bf16[256,5120]{1,0:T(8,128)(2,1)S(1)}, bf16[256,5120]{1,0:T(8,128)(2,1)}, u32[]{:S(2)}) copy-start(bf16[256,5120]{1,0:T(8,128)(2,1)} %param.6) | copy-start | bytes 7864324
  3.7 11.0 %copy-start.1 = (bf16[320,3072]{1,0:T(8,128)(2,1)}, bf16[320,3072]{1,0:T(8,128)(2,1)S(1)}, u32[]{:S(2)}) copy-start(bf16[320,3072]{1,0:T(8,128)(2,1)S(1)} %pad_maximum_fusion.1.refs_4_.refs_2_.refs_1_.refs_3_) | copy-start | bytes 5898244
  3.7 10.2 %copy-start.24 = (f32[5120]{0:T(1024)S(1)}, f32[5120]{0:T(1024)}, u32[]{:S(2)}) copy-start(f32[5120]{0:T(1024)} %param.8) | copy-start | bytes 61444
  3.7 51.4 %collective-permute-start.3 = (bf16[320,3072]{1,0:T(8,128)(2,1)S(1)}, bf16[320,3072]{1,0:T(8,128)(2,1)S(1)}, u32[]{:S(2)}, u32[]{:S(2)}) collective-permute-start(bf16[320,3072]{1,0:T(8,128)(2,1)S(1)} %pad_maximum_fusion.1.refs_4_.refs_2_.refs_1_.refs_3_), channel_id=1, source_target_pairs={{0,1},{3,2},{4,5},{7,6},{8,9},{11,10},{12,13},{15,14},{16,17},{19,... | collective-permute-start | bytes 5898248 | tf_op jit(solution)/shard_map/ppermute | solution.py:289
  11.7 44.6 %collective-permute-start.7 = (bf16[320,3072]{1,0:T(8,128)(2,1)S(1)}, bf16[320,3072]{1,0:T(8,128)(2,1)S(1)}, u32[]{:S(2)}, u32[]{:S(2)}) collective-permute-start(bf16[320,3072]{1,0:T(8,128)(2,1)S(1)} %pad_maximum_fusion.1.refs_4_.refs_2_.refs_1_.refs_3_), channel_id=1, source_target_pairs={{0,8},{4,12},{8,0},{12,4},{1,9},{5,13},{9,1},{13,5},{2,10},{6,14},... | collective-permute-start | bytes 5898248 | tf_op jit(solution)/shard_map/ppermute | solution.py:292
  13.3 88.5 %collective-permute-start.14 = (bf16[320,3072]{1,0:T(8,128)(2,1)S(1)}, bf16[320,3072]{1,0:T(8,128)(2,1)S(1)}, u32[]{:S(2)}, u32[]{:S(2)}) collective-permute-start(bf16[320,3072]{1,0:T(8,128)(2,1)S(1)} %pad_maximum_fusion.1.refs_4_.refs_2_.refs_1_.refs_3_), channel_id=1, source_target_pairs={{0,4},{4,0},{8,12},{12,8},{1,5},{5,1},{9,13},{13,9},{2,6},{6,2},{1... | collective-permute-start | bytes 5898248 | tf_op jit(solution)/shard_map/ppermute | solution.py:292
  14.7 106.6 %copy-start.7 = (bf16[256,5120]{1,0:T(8,128)(2,1)}, bf16[256,5120]{1,0:T(8,128)(2,1)S(1)}, u32[]{:S(2)}) copy-start(bf16[256,5120]{1,0:T(8,128)(2,1)S(1)} %fusion.2.refs_0_) | copy-start | bytes 7864324
  14.7 112.7 %copy-start = (bf16[320,3072]{1,0:T(8,128)(2,1)}, bf16[320,3072]{1,0:T(8,128)(2,1)S(1)}, u32[]{:S(2)}) copy-start(bf16[320,3072]{1,0:T(8,128)(2,1)S(1)} %collective-permute-done.refs_6_.refs_4_.refs_3_.refs_5_) | copy-start | bytes 5898244
  14.8 62.5 %collective-permute-start.1 = (bf16[320,1536]{1,0:T(8,128)(2,1)S(1)}, bf16[320,1536]{1,0:T(8,128)(2,1)S(1)}, u32[]{:S(2)}, u32[]{:S(2)}) collective-permute-start(bf16[320,1536]{1,0:T(8,128)(2,1)S(1)} %get-tuple-element.27), channel_id=1, source_target_pairs={{0,2},{3,1},{4,6},{7,5},{8,10},{11,9},{12,14},{15,13},{16,18},{19,... | collective-permute-start | bytes 2949128 | tf_op jit(solution)/shard_map/ppermute | solution.py:289
  55.1 46.2 %copy-start.2 = (bf16[320,3072]{1,0:T(8,128)(2,1)}, bf16[320,3072]{1,0:T(8,128)(2,1)S(1)}, u32[]{:S(2)}) copy-start(bf16[320,3072]{1,0:T(8,128)(2,1)S(1)} %collective-permute-done.3.refs_5_.refs_3_.refs_2_.refs_4_) | copy-start | bytes 5898244
  56.4 44.9 %copy-start.3 = (bf16[320,3072]{1,0:T(8,128)(2,1)}, bf16[320,3072]{1,0:T(8,128)(2,1)S(1)}, u32[]{:S(2)}) copy-start(bf16[320,3072]{1,0:T(8,128)(2,1)S(1)} %collective-permute-done.7.refs_8_.refs_6_.refs_5_.refs_7_) | copy-start | bytes 5898244
  56.4 24.7 %collective-permute-start.9 = (bf16[320,1536]{1,0:T(8,128)(2,1)S(1)}, bf16[320,1536]{1,0:T(8,128)(2,1)S(1)}, u32[]{:S(2)}, u32[]{:S(2)}) collective-permute-start(bf16[320,1536]{1,0:T(8,128)(2,1)S(1)} %get-tuple-element.33), channel_id=1, source_target_pairs={{0,8},{4,12},{8,0},{12,4},{1,9},{5,13},{9,1},{13,5},{2,10},{6,14},... | collective-permute-start | bytes 2949128 | tf_op jit(solution)/shard_map/ppermute | solution.py:292
  58.0 121.5 %copy-start.25 = (f32[128]{0:T(128)S(1)}, f32[128]{0:T(128)}, u32[]{:S(2)}) copy-start(f32[128]{0:T(128)} %param.10) | copy-start | bytes 1540
  58.0 121.5 %copy-start.26 = (f32[128]{0:T(128)S(1)}, f32[128]{0:T(128)}, u32[]{:S(2)}) copy-start(f32[128]{0:T(128)} %param.9) | copy-start | bytes 1540
  58.0 41.7 %collective-permute-start.8 = (bf16[320,1536]{1,0:T(8,128)(2,1)S(1)}, bf16[320,1536]{1,0:T(8,128)(2,1)S(1)}, u32[]{:S(2)}, u32[]{:S(2)}) collective-permute-start(bf16[320,1536]{1,0:T(8,128)(2,1)S(1)} %get-tuple-element.32), channel_id=1, source_target_pairs={{0,8},{4,12},{8,0},{12,4},{1,9},{5,13},{9,1},{13,5},{2,10},{6,14},... | collective-permute-start | bytes 2949128 | tf_op jit(solution)/shard_map/ppermute | solution.py:292
  58.8 44.4 %collective-permute-start.4 = (bf16[128,5120]{1,0:T(8,128)(2,1)S(1)}, bf16[128,5120]{1,0:T(8,128)(2,1)}, u32[]{:S(2)}, u32[]{:S(2)}) collective-permute-start(bf16[128,5120]{1,0:T(8,128)(2,1)S(1)} %get-tuple-element.29), channel_id=1, source_target_pairs={{0,1},{3,2},{4,5},{7,6},{8,9},{11,10},{12,13},{15,14},{16,17},{19,... | collective-permute-start | bytes 3932168 | tf_op jit(solution)/shard_map/ppermute | solution.py:289
  77.2 106.8 %copy-start.8 = (bf16[320,1536]{1,0:T(8,128)(2,1)}, bf16[320,1536]{1,0:T(8,128)(2,1)S(1)}, u32[]{:S(2)}) copy-start(bf16[320,1536]{1,0:T(8,128)(2,1)S(1)} %collective-permute-done.1.refs_4_.refs_6_) | copy-start | bytes 2949124
  81.0 92.3 %copy-start.9 = (bf16[320,1536]{1,0:T(8,128)(2,1)}, bf16[320,1536]{1,0:T(8,128)(2,1)S(1)}, u32[]{:S(2)}) copy-start(bf16[320,1536]{1,0:T(8,128)(2,1)S(1)} %collective-permute-done.9.refs_6_.refs_8_) | copy-start | bytes 2949124
  99.8 75.5 %copy-start.10 = (bf16[320,1536]{1,0:T(8,128)(2,1)}, bf16[320,1536]{1,0:T(8,128)(2,1)S(1)}, u32[]{:S(2)}) copy-start(bf16[320,1536]{1,0:T(8,128)(2,1)S(1)} %collective-permute-done.8.refs_7_.refs_9_) | copy-start | bytes 2949124
  99.8 21.5 %collective-permute-start.10 = (bf16[320,1536]{1,0:T(8,128)(2,1)S(1)}, bf16[320,1536]{1,0:T(8,128)(2,1)}, u32[]{:S(2)}, u32[]{:S(2)}) collective-permute-start(bf16[320,1536]{1,0:T(8,128)(2,1)S(1)} %collective-permute-done.1.refs_4_.refs_6_), channel_id=1, source_target_pairs={{0,8},{4,12},{8,0},{12,4},{1,9},{5,13},{9,1},{13,5},{2,10},{6,14},... | collective-permute-start | bytes 2949128 | tf_op jit(solution)/shard_map/ppermute | solution.py:292
  101.3 26.3 %collective-permute-start.15 = (bf16[320,3072]{1,0:T(8,128)(2,1)S(1)}, bf16[320,3072]{1,0:T(8,128)(2,1)S(1)}, u32[]{:S(2)}, u32[]{:S(2)}) collective-permute-start(bf16[320,3072]{1,0:T(8,128)(2,1)S(1)} %collective-permute-done.3.refs_5_.refs_3_.refs_2_.refs_4_), channel_id=1, source_target_pairs={{0,4},{4,0},{8,12},{12,8},{1,5},{5,1},{9,13},{13,9},{2,6},{6,2},{1... | collective-permute-start | bytes 5898248 | tf_op jit(solution)/shard_map/ppermute | solution.py:292
  101.3 28.7 %collective-permute-start.18 = (bf16[320,3072]{1,0:T(8,128)(2,1)S(1)}, bf16[320,3072]{1,0:T(8,128)(2,1)S(1)}, u32[]{:S(2)}, u32[]{:S(2)}) collective-permute-start(bf16[320,3072]{1,0:T(8,128)(2,1)S(1)} %collective-permute-done.7.refs_8_.refs_6_.refs_5_.refs_7_), channel_id=1, source_target_pairs={{0,4},{4,0},{8,12},{12,8},{1,5},{5,1},{9,13},{13,9},{2,6},{6,2},{1... | collective-permute-start | bytes 5898248 | tf_op jit(solution)/shard_map/ppermute | solution.py:292
  101.8 28.2 %copy-start.4 = (bf16[320,3072]{1,0:T(8,128)(2,1)}, bf16[320,3072]{1,0:T(8,128)(2,1)S(1)}, u32[]{:S(2)}) copy-start(bf16[320,3072]{1,0:T(8,128)(2,1)S(1)} %collective-permute-done.14.refs_12_.refs_10_.refs_9_.refs_11_) | copy-start | bytes 5898244
  101.8 20.3 %collective-permute-start.25 = (bf16[320,1536]{1,0:T(8,128)(2,1)S(1)}, bf16[320,1536]{1,0:T(8,128)(2,1)S(1)}, u32[]{:S(2)}, u32[]{:S(2)}) collective-permute-start(bf16[320,1536]{1,0:T(8,128)(2,1)S(1)} %collective-permute-done.9.refs_6_.refs_8_), channel_id=1, source_target_pairs={{0,4},{4,0},{8,12},{12,8},{1,5},{5,1},{9,13},{13,9},{2,6},{6,2},{1... | collective-permute-start | bytes 2949128 | tf_op jit(solution)/shard_map/ppermute | solution.py:292
  103.2 24.2 %collective-permute-start.26 = (bf16[320,1536]{1,0:T(8,128)(2,1)S(1)}, bf16[320,1536]{1,0:T(8,128)(2,1)S(1)}, u32[]{:S(2)}, u32[]{:S(2)}) collective-permute-start(bf16[320,1536]{1,0:T(8,128)(2,1)S(1)} %collective-permute-done.8.refs_7_.refs_9_), channel_id=1, source_target_pairs={{0,4},{4,0},{8,12},{12,8},{1,5},{5,1},{9,13},{13,9},{2,6},{6,2},{1... | collective-permute-start | bytes 2949128 | tf_op jit(solution)/shard_map/ppermute | solution.py:292
  121.3 52.0 %collective-permute-start.2 = (bf16[256,5120]{1,0:T(8,128)(2,1)S(1)}, bf16[256,5120]{1,0:T(8,128)(2,1)S(1)}, u32[]{:S(2)}, u32[]{:S(2)}) collective-permute-start(bf16[256,5120]{1,0:T(8,128)(2,1)S(1)} %fusion.2.refs_0_), channel_id=1, source_target_pairs={{1,2},{2,1},{5,6},{6,5},{9,10},{10,9},{13,14},{14,13},{17,18},{18,... | collective-permute-start | bytes 7864328 | tf_op jit(solution)/shard_map/ppermute | solution.py:289
  122.1 53.2 %copy-start.11 = (bf16[320,1536]{1,0:T(8,128)(2,1)}, bf16[320,1536]{1,0:T(8,128)(2,1)S(1)}, u32[]{:S(2)}) copy-start(bf16[320,1536]{1,0:T(8,128)(2,1)S(1)} %collective-permute-done.25.refs_14_.refs_16_) | copy-start | bytes 2949124
  122.1 27.4 %collective-permute-start.6 = (bf16[320,1536]{1,0:T(8,128)(2,1)S(1)}, bf16[320,1536]{1,0:T(8,128)(2,1)S(1)}, u32[]{:S(2)}, u32[]{:S(2)}) collective-permute-start(bf16[320,1536]{1,0:T(8,128)(2,1)S(1)} %get-tuple-element.31), channel_id=1, source_target_pairs={{0,2},{3,1},{4,6},{7,5},{8,10},{11,9},{12,14},{15,13},{16,18},{19,... | collective-permute-start | bytes 2949128 | tf_op jit(solution)/shard_map/ppermute | solution.py:289
  127.5 47.9 %copy-start.12 = (bf16[320,1536]{1,0:T(8,128)(2,1)}, bf16[320,1536]{1,0:T(8,128)(2,1)S(1)}, u32[]{:S(2)}) copy-start(bf16[320,1536]{1,0:T(8,128)(2,1)S(1)} %collective-permute-done.26.refs_15_.refs_17_) | copy-start | bytes 2949124
  127.5 53.7 %collective-permute-start.16 = (bf16[320,3072]{1,0:T(8,128)(2,1)S(1)}, bf16[320,3072]{1,0:T(8,128)(2,1)}, u32[]{:S(2)}, u32[]{:S(2)}) collective-permute-start(bf16[320,3072]{1,0:T(8,128)(2,1)S(1)} %collective-permute-done.refs_6_.refs_4_.refs_3_.refs_5_), channel_id=1, source_target_pairs={{0,4},{4,0},{8,12},{12,8},{1,5},{5,1},{9,13},{13,9},{2,6},{6,2},{1... | collective-permute-start | bytes 5898248 | tf_op jit(solution)/shard_map/ppermute | solution.py:292
  127.6 3.9 %copy-start.5 = (bf16[320,3072]{1,0:T(8,128)(2,1)}, bf16[320,3072]{1,0:T(8,128)(2,1)S(1)}, u32[]{:S(2)}) copy-start(bf16[320,3072]{1,0:T(8,128)(2,1)S(1)} %collective-permute-done.15.refs_13_.refs_11_.refs_10_.refs_12_) | copy-start | bytes 5898244
  127.6 45.7 %collective-permute-start.5 = (bf16[128,5120]{1,0:T(8,128)(2,1)S(1)}, bf16[128,5120]{1,0:T(8,128)(2,1)}, u32[]{:S(2)}, u32[]{:S(2)}) collective-permute-start(bf16[128,5120]{1,0:T(8,128)(2,1)S(1)} %get-tuple-element.30), channel_id=1, source_target_pairs={{0,1},{3,2},{4,5},{7,6},{8,9},{11,10},{12,13},{15,14},{16,17},{19,... | collective-permute-start | bytes 3932168 | tf_op jit(solution)/shard_map/ppermute | solution.py:289
  130.0 19.6 %copy-start.6 = (bf16[320,3072]{1,0:T(8,128)(2,1)}, bf16[320,3072]{1,0:T(8,128)(2,1)S(1)}, u32[]{:S(2)}) copy-start(bf16[320,3072]{1,0:T(8,128)(2,1)S(1)} %collective-permute-done.18.refs_16_.refs_14_.refs_13_.refs_15_) | copy-start | bytes 5898244
  130.0 45.3 %collective-permute-start.12 = (bf16[320,1536]{1,0:T(8,128)(2,1)S(1)}, bf16[320,1536]{1,0:T(8,128)(2,1)S(1)}, u32[]{:S(2)}, u32[]{:S(2)}) collective-permute-start(bf16[320,1536]{1,0:T(8,128)(2,1)S(1)} %get-tuple-element.36), channel_id=1, source_target_pairs={{0,8},{4,12},{8,0},{12,4},{1,9},{5,13},{9,1},{13,5},{2,10},{6,14},... | collective-permute-start | bytes 2949128 | tf_op jit(solution)/shard_map/ppermute | solution.py:292
  149.6 25.7 %copy-start.15 = (bf16[320,1536]{1,0:T(8,128)(2,1)}, bf16[320,1536]{1,0:T(8,128)(2,1)S(1)}, u32[]{:S(2)}) copy-start(bf16[320,1536]{1,0:T(8,128)(2,1)S(1)} %collective-permute-done.6.refs_7_.refs_5_) | copy-start | bytes 2949124
  149.6 30.0 %collective-permute-start.24 = (bf16[320,1536]{1,0:T(8,128)(2,1)S(1)}, bf16[320,1536]{1,0:T(8,128)(2,1)}, u32[]{:S(2)}, u32[]{:S(2)}) collective-permute-start(bf16[320,1536]{1,0:T(8,128)(2,1)S(1)} %collective-permute-done.1.refs_4_.refs_6_), channel_id=1, source_target_pairs={{0,4},{4,0},{8,12},{12,8},{1,5},{5,1},{9,13},{13,9},{2,6},{6,2},{1... | collective-permute-start | bytes 2949128 | tf_op jit(solution)/shard_map/ppermute | solution.py:292
  173.3 10.6 %collective-permute-start.27 = (bf16[320,1536]{1,0:T(8,128)(2,1)}, bf16[320,1536]{1,0:T(8,128)(2,1)}, u32[]{:S(2)}, u32[]{:S(2)}) collective-permute-start(bf16[320,1536]{1,0:T(8,128)(2,1)} %collective-permute-done.10.refs_8_.refs_10_), channel_id=1, source_target_pairs={{0,4},{4,0},{8,12},{12,8},{1,5},{5,1},{9,13},{13,9},{2,6},{6,2},{1... | collective-permute-start | bytes 2949128 | tf_op jit(solution)/shard_map/ppermute | solution.py:292
  173.3 2.0 copy-start.14
  173.3 31.1 %collective-permute-start.22 = (bf16[128,5120]{1,0:T(8,128)(2,1)}, bf16[128,5120]{1,0:T(8,128)(2,1)}, u32[]{:S(2)}, u32[]{:S(2)}) collective-permute-start(bf16[128,5120]{1,0:T(8,128)(2,1)} %collective-permute-done.4.refs_2_.refs_1_), channel_id=1, source_target_pairs={{1,2},{2,1},{5,6},{6,5},{9,10},{10,9},{13,14},{14,13},{17,18},{18,... | collective-permute-start | bytes 3932168 | tf_op jit(solution)/shard_map/ppermute | solution.py:289
  175.3 0.9 copy-start.17
  176.3 58.6 %collective-permute-start.23 = (bf16[128,5120]{1,0:T(8,128)(2,1)}, bf16[128,5120]{1,0:T(8,128)(2,1)}, u32[]{:S(2)}, u32[]{:S(2)}) collective-permute-start(bf16[128,5120]{1,0:T(8,128)(2,1)} %collective-permute-done.5.refs_3_.refs_2_), channel_id=1, source_target_pairs={{1,2},{2,1},{5,6},{6,5},{9,10},{10,9},{13,14},{14,13},{17,18},{18,... | collective-permute-start | bytes 3932168 | tf_op jit(solution)/shard_map/ppermute | solution.py:289
  179.6 24.8 %collective-permute-start.11 = (bf16[320,1536]{1,0:T(8,128)(2,1)}, bf16[320,1536]{1,0:T(8,128)(2,1)S(1)}, u32[]{:S(2)}, u32[]{:S(2)}) collective-permute-start(bf16[320,1536]{1,0:T(8,128)(2,1)} %get-tuple-element.35), channel_id=1, source_target_pairs={{0,8},{4,12},{8,0},{12,4},{1,9},{5,13},{9,1},{13,5},{2,10},{6,14},... | collective-permute-start | bytes 2949128 | tf_op jit(solution)/shard_map/ppermute | solution.py:292
  181.1 43.9 %collective-permute-start.13 = (bf16[320,1536]{1,0:T(8,128)(2,1)}, bf16[320,1536]{1,0:T(8,128)(2,1)S(1)}, u32[]{:S(2)}, u32[]{:S(2)}) collective-permute-start(bf16[320,1536]{1,0:T(8,128)(2,1)} %copy-done.15), channel_id=1, source_target_pairs={{0,8},{4,12},{8,0},{12,4},{1,9},{5,13},{9,1},{13,5},{2,10},{6,14},... | collective-permute-start | bytes 2949128 | tf_op jit(solution)/shard_map/ppermute | solution.py:292
  181.7 2.3 copy-start.16
  183.9 80.9 %collective-permute-start.17 = (bf16[320,1536]{1,0:T(8,128)(2,1)S(1)}, bf16[320,1536]{1,0:T(8,128)(2,1)S(1)}, u32[]{:S(2)}, u32[]{:S(2)}) collective-permute-start(bf16[320,1536]{1,0:T(8,128)(2,1)S(1)} %copy-done.16), channel_id=1, source_target_pairs={{0,4},{4,0},{8,12},{12,8},{1,5},{5,1},{9,13},{13,9},{2,6},{6,2},{1... | collective-permute-start | bytes 2949128 | tf_op jit(solution)/shard_map/ppermute | solution.py:292
  184.0 20.4 %copy-start.18 = (bf16[320,1536]{1,0:T(8,128)(2,1)S(1)}, bf16[320,1536]{1,0:T(8,128)(2,1)}, u32[]{:S(2)}) copy-start(bf16[320,1536]{1,0:T(8,128)(2,1)} %copy-done.17) | copy-start | bytes 2949124
  204.4 30.5 %copy-start.19 = (bf16[320,1536]{1,0:T(8,128)(2,1)}, bf16[320,1536]{1,0:T(8,128)(2,1)S(1)}, u32[]{:S(2)}) copy-start(bf16[320,1536]{1,0:T(8,128)(2,1)S(1)} %collective-permute-done.11.refs_9_.refs_7_) | copy-start | bytes 2949124
  204.4 68.3 %collective-permute-start.20 = (bf16[320,1536]{1,0:T(8,128)(2,1)S(1)}, bf16[320,1536]{1,0:T(8,128)(2,1)S(1)}, u32[]{:S(2)}, u32[]{:S(2)}) collective-permute-start(bf16[320,1536]{1,0:T(8,128)(2,1)S(1)} %copy-done.18), channel_id=1, source_target_pairs={{0,4},{4,0},{8,12},{12,8},{1,5},{5,1},{9,13},{13,9},{2,6},{6,2},{1... | collective-permute-start | bytes 2949128 | tf_op jit(solution)/shard_map/ppermute | solution.py:292
  204.4 69.6 %collective-permute-start.19 = (bf16[320,1536]{1,0:T(8,128)(2,1)S(1)}, bf16[320,1536]{1,0:T(8,128)(2,1)S(1)}, u32[]{:S(2)}, u32[]{:S(2)}) collective-permute-start(bf16[320,1536]{1,0:T(8,128)(2,1)S(1)} %collective-permute-done.11.refs_9_.refs_7_), channel_id=1, source_target_pairs={{0,4},{4,0},{8,12},{12,8},{1,5},{5,1},{9,13},{13,9},{2,6},{6,2},{1... | collective-permute-start | bytes 2949128 | tf_op jit(solution)/shard_map/ppermute | solution.py:292
  225.1 9.8 %copy-start.20 = (bf16[320,1536]{1,0:T(8,128)(2,1)}, bf16[320,1536]{1,0:T(8,128)(2,1)S(1)}, u32[]{:S(2)}) copy-start(bf16[320,1536]{1,0:T(8,128)(2,1)S(1)} %collective-permute-done.13.refs_11_.refs_9_) | copy-start | bytes 2949124
  225.1 50.2 %collective-permute-start.21 = (bf16[320,1536]{1,0:T(8,128)(2,1)S(1)}, bf16[320,1536]{1,0:T(8,128)(2,1)}, u32[]{:S(2)}, u32[]{:S(2)}) collective-permute-start(bf16[320,1536]{1,0:T(8,128)(2,1)S(1)} %collective-permute-done.13.refs_11_.refs_9_), channel_id=1, source_target_pairs={{0,4},{4,0},{8,12},{12,8},{1,5},{5,1},{9,13},{13,9},{2,6},{6,2},{1... | collective-permute-start | bytes 2949128 | tf_op jit(solution)/shard_map/ppermute | solution.py:292
  234.9 36.5 %collective-permute-start.32 = (bf16[128,1536]{1,0:T(8,128)(2,1)S(1)}, bf16[128,1536]{1,0:T(8,128)(2,1)S(1)}, u32[]{:S(2)}, u32[]{:S(2)}) collective-permute-start(bf16[128,1536]{1,0:T(8,128)(2,1)S(1)} %project.10), channel_id=1, source_target_pairs={{1,0},{2,3},{5,4},{6,7},{9,8},{10,11},{13,12},{14,15},{17,16},{18,... | collective-permute-start | bytes 1179656 | tf_op jit(solution)/shard_map/ppermute | solution.py:289
  255.0 16.3 %copy-start.27 = (bf16[256,1536]{1,0:T(8,128)(2,1)S(1)}, bf16[256,1536]{1,0:T(8,128)(2,1)}, u32[]{:S(2)}) copy-start(bf16[256,1536]{1,0:T(8,128)(2,1)} %get-tuple-element.46) | copy-start | bytes 2359300
  264.9 12.0 %copy-start.21 = (bf16[320,1536]{1,0:T(8,128)(2,1)}, bf16[320,1536]{1,0:T(8,128)(2,1)S(1)}, u32[]{:S(2)}) copy-start(bf16[320,1536]{1,0:T(8,128)(2,1)S(1)} %collective-permute-done.17.refs_15_.refs_13_) | copy-start | bytes 2949124
  264.9 50.0 %collective-permute-start.28 = (bf16[256,1536]{1,0:T(8,128)(2,1)S(1)}, bf16[256,1536]{1,0:T(8,128)(2,1)}, u32[]{:S(2)}, u32[]{:S(2)}) collective-permute-start(bf16[256,1536]{1,0:T(8,128)(2,1)S(1)} %project.8), channel_id=1, source_target_pairs={{1,0},{2,3},{5,4},{6,7},{9,8},{10,11},{13,12},{14,15},{17,16},{18,... | collective-permute-start | bytes 2359304 | tf_op jit(solution)/shard_map/ppermute | solution.py:289
  271.3 31.8 %copy-start.28 = (bf16[128,1536]{1,0:T(8,128)(2,1)}, bf16[128,1536]{1,0:T(8,128)(2,1)S(1)}, u32[]{:S(2)}) copy-start(bf16[128,1536]{1,0:T(8,128)(2,1)S(1)} %collective-permute-done.32.refs_10_) | copy-start | bytes 1179652
  271.3 72.3 %collective-permute-start.29 = (bf16[256,1536]{1,0:T(8,128)(2,1)S(1)}, bf16[256,1536]{1,0:T(8,128)(2,1)}, u32[]{:S(2)}, u32[]{:S(2)}) collective-permute-start(bf16[256,1536]{1,0:T(8,128)(2,1)S(1)} %copy-done.27), channel_id=1, source_target_pairs={{1,0},{2,3},{5,4},{6,7},{9,8},{10,11},{13,12},{14,15},{17,16},{18,... | collective-permute-start | bytes 2359304 | tf_op jit(solution)/shard_map/ppermute | solution.py:289
  272.6 4.2 %copy-start.22 = (bf16[320,1536]{1,0:T(8,128)(2,1)}, bf16[320,1536]{1,0:T(8,128)(2,1)S(1)}, u32[]{:S(2)}) copy-start(bf16[320,1536]{1,0:T(8,128)(2,1)S(1)} %collective-permute-done.20.refs_18_.refs_16_) | copy-start | bytes 2949124
  272.7 62.6 %collective-permute-start.30 = (bf16[128,1536]{1,0:T(8,128)(2,1)S(1)}, bf16[128,1536]{1,0:T(8,128)(2,1)S(1)}, u32[]{:S(2)}, u32[]{:S(2)}) collective-permute-start(bf16[128,1536]{1,0:T(8,128)(2,1)S(1)} %get-tuple-element.47), channel_id=1, source_target_pairs={{1,0},{2,3},{5,4},{6,7},{9,8},{10,11},{13,12},{14,15},{17,16},{18,... | collective-permute-start | bytes 1179656 | tf_op jit(solution)/shard_map/ppermute | solution.py:289
  274.0 1.3 copy-start.23
  274.0 69.7 %collective-permute-start.31 = (bf16[128,1536]{1,0:T(8,128)(2,1)S(1)}, bf16[128,1536]{1,0:T(8,128)(2,1)S(1)}, u32[]{:S(2)}, u32[]{:S(2)}) collective-permute-start(bf16[128,1536]{1,0:T(8,128)(2,1)S(1)} %get-tuple-element.48), channel_id=1, source_target_pairs={{1,0},{2,3},{5,4},{6,7},{9,8},{10,11},{13,12},{14,15},{17,16},{18,... | collective-permute-start | bytes 1179656 | tf_op jit(solution)/shard_map/ppermute | solution.py:289
  275.3 76.6 %collective-permute-start.33 = (bf16[128,1536]{1,0:T(8,128)(2,1)S(1)}, bf16[128,1536]{1,0:T(8,128)(2,1)S(1)}, u32[]{:S(2)}, u32[]{:S(2)}) collective-permute-start(bf16[128,1536]{1,0:T(8,128)(2,1)S(1)} %project.11), channel_id=1, source_target_pairs={{1,0},{2,3},{5,4},{6,7},{9,8},{10,11},{13,12},{14,15},{17,16},{18,... | collective-permute-start | bytes 1179656 | tf_op jit(solution)/shard_map/ppermute | solution.py:289
  343.7 8.2 %copy-start.29 = (bf16[128,1536]{1,0:T(8,128)(2,1)}, bf16[128,1536]{1,0:T(8,128)(2,1)S(1)}, u32[]{:S(2)}) copy-start(bf16[128,1536]{1,0:T(8,128)(2,1)S(1)} %collective-permute-done.31.refs_9_) | copy-start | bytes 1179652
  (1 other events, 0.7 us)
